TPU v7x, 32 devices: a whole 2x2x4 slice. The times are simulated.
32 devices in a mesh: head: 4 (over y, x), node: 8 (over z, core).
Axes of the slice: x: 2, y: 2, z: 4, core: 2. Of those that a mesh axis runs over, the one named last changes fastest.
Arguments:
- prev_state: float32 [98304, 84], P('node'), may hold values from -6 to 6
- target: float32 [98304, 84], P('node')
- noise_eps: float32 [98304, 84], P('node'), may hold values from -6 to 6
- noise_level: int32 [1], replicated, may hold values from 0 to 999
- valid_count: int32 [8], P('node'), may hold values from 1 to 2048, as said below
- neighbours: int32 [16384, 16], P('node'), may hold values from 0 to 16383, as said below
- nbr_count: int32 [16384], P('node'), may hold values from 8 to 16
- pix_node: int32 [98304], P('node'), may hold values from 0 to 16383, as said below
- pix_read: int32 [98304, 3], P('node'), may hold values from 0 to 16383, as said below
- w_enc: float32 [168, 512], replicated, may hold values from -0.1875 to 0.1875
- w_cond: float32 [32, 2048], replicated, may hold values from -1 to 1
- w_dec: float32 [512, 84], replicated, may hold values from -0.25 to 0.25
- layer_w: float32 [3, 512, 2048], P(None, 'node', 'head'), may hold values from -0.25 to 0.25
- soap_first: float32 [3, 512, 2048], P(None, 'node', 'head'), may hold values from -9.536743e-06 to 9.536743e-06
- soap_second: float32 [3, 512, 2048], P(None, 'node', 'head'), may hold values from 1.57566e-12 to 6.30264e-12
- soap_basis: float32 [3, 4, 512, 512], P(None, 'head')
- soap_stats: float32 [3, 4, 512, 512], P(None, 'head')
- enc_first: float32 [168, 512], replicated, may hold values from -9.536743e-06 to 9.536743e-06
- enc_second: float32 [168, 512], replicated, may hold values from 1.57566e-12 to 6.30264e-12
- cond_first: float32 [32, 2048], replicated, may hold values from -9.536743e-06 to 9.536743e-06
- cond_second: float32 [32, 2048], replicated, may hold values from 1.57566e-12 to 6.30264e-12
- dec_first: float32 [512, 84], replicated, may hold values from -9.536743e-06 to 9.536743e-06
- dec_second: float32 [512, 84], replicated, may hold values from 1.57566e-12 to 6.30264e-12
Outputs:
- loss_sum: float32 [1], replicated
- loss_count: float32 [1], replicated
- grad_norm: float32 [1], replicated
- layer_w_new: float32 [3, 512, 2048], P(None, 'node', 'head')
- soap_first_new: float32 [3, 512, 2048], P(None, 'node', 'head')
- soap_second_new: float32 [3, 512, 2048], P(None, 'node', 'head')
- soap_basis_new: float32 [3, 4, 512, 512], P(None, 'head')
- soap_stats_new: float32 [3, 4, 512, 512], P(None, 'head')
- w_enc_new: float32 [168, 512], replicated
- enc_first_new: float32 [168, 512], replicated
- enc_second_new: float32 [168, 512], replicated
- w_cond_new: float32 [32, 2048], replicated
- cond_first_new: float32 [32, 2048], replicated
- cond_second_new: float32 [32, 2048], replicated
- w_dec_new: float32 [512, 84], replicated
- dec_first_new: float32 [512, 84], replicated
- dec_second_new: float32 [512, 84], replicated
Inputs may be any that keep to these rules, and one draw needn't show every extreme that they name: `pix_node`: pixel p encodes into a node of block p // 12288 of 2048 nodes. `pix_read`: pixel p reads three nodes of block p // 12288. The neighbours of a node of block b lie in blocks b - 1, b and b + 1 of 2048 nodes, cyclically. `valid_count`: the last block's nodes are all valid.
All inputs are finite; a program needn't handle non-finite values.
Results may differ from a plain program's by a relative error of at most 0.0074.
Values may be sent and summed in bfloat16 or wider, within the bound.
A program may use at most 320 MiB of HBM per device.

v0:
```python
import math

import jax
import jax.numpy as jnp
from jax import lax
from jax.sharding import PartitionSpec as P

HD = 128
VARS = 84
NF = 32
NBR = 16
LEVELS = 1000
STEP = 10


highest = lax.Precision.HIGHEST
clip_limit = 0.01
beta_first = 0.9
beta_second = 0.95
beta_stats = 0.95
adam_epsilon = 1e-08
rate_layer = 0.02
rate_small = 0.05
decay_rate = 0.1
norm_eps = 1e-05


def extended(block, sides, width):
    for axis, dim in sides:
        count = lax.axis_size(axis)
        forward = [(i, i + 1) for i in range(count - 1)]
        forward.append((count - 1, 0))
        backward = [(target, source) for source, target in forward]
        low = lax.ppermute(
            lax.slice_in_dim(block, block.shape[dim] - width, None, axis=dim), axis, forward
        )
        high = lax.ppermute(lax.slice_in_dim(block, 0, width, axis=dim), axis, backward)
        block = jnp.concatenate([low, block, high], axis=dim)
    return block


def passed_along(x, axis, by):
    length = lax.axis_size(axis)
    return lax.ppermute(x, axis, [(i, (i + by) % length) for i in range(length)])


def noise_terms(noise_level):
    level_frac = noise_level[0].astype(jnp.float32) / (LEVELS - 1)
    noise_sigma = 0.05 * jnp.exp(level_frac * math.log(40.0))
    frequency = 1.0 + jnp.arange(NF // 2).astype(jnp.float32)
    phase_angle = jnp.log(noise_sigma) * frequency
    return (noise_sigma, jnp.concatenate([jnp.sin(phase_angle), jnp.cos(phase_angle)]))


def standardize(values_in):
    row_mean = jnp.mean(values_in, -1, keepdims=True)
    centered = values_in - row_mean
    inv_std = lax.rsqrt(jnp.mean(centered * centered, -1, keepdims=True) + norm_eps)
    return (centered * inv_std, inv_std)


def norm_back(normed, inv_std, grad_in):
    return inv_std * (
        grad_in
        - jnp.mean(grad_in, -1, keepdims=True)
        - normed * jnp.mean(grad_in * normed, -1, keepdims=True)
    )


def contract(left, right, left_dim, right_dim):
    return lax.dot_general(
        left, right, (((left_dim,), (right_dim,)), ((), ())), preferred_element_type=jnp.float32
    )


def adam_small(weight, grad_item, first, second):
    first_new = beta_first * first + (1 - beta_first) * grad_item
    second_new = beta_second * second + (1 - beta_second) * grad_item * grad_item
    ratio = (
        first_new
        / (1 - beta_first**STEP)
        / (jnp.sqrt(second_new / (1 - beta_second**STEP)) + adam_epsilon)
    )
    return (weight - rate_small * (ratio + decay_rate * weight), first_new, second_new)


def local(
    prev_state,
    target,
    noise_eps,
    noise_level,
    valid_count,
    neighbours,
    nbr_count,
    pix_node,
    pix_read,
    w_enc,
    w_cond,
    w_dec,
    layer_w,
    soap_first,
    soap_second,
    soap_basis,
    soap_stats,
    enc_first,
    enc_second,
    cond_first,
    cond_second,
    dec_first,
    dec_second,
):
    node_rows = nbr_count.shape[0]
    groups = lax.axis_size("node")
    block_start = lax.axis_index("node") * node_rows
    model_width = w_enc.shape[1]
    weights = lax.all_gather(layer_w.astype(jnp.bfloat16), "node", axis=1, tiled=True)
    block_cols = weights.shape[2]
    heads_here = block_cols // (4 * HD)
    attn_w = weights[0].reshape(model_width, heads_here, 4, HD)
    w_qkv = attn_w[:, :, :3, :].reshape(model_width, heads_here * 3 * HD)
    w_out = attn_w[:, :, 3, :].reshape(model_width, heads_here * HD)
    w_up = weights[1]
    w_down = weights[2]
    noise_sigma, noise_feat = noise_terms(noise_level)
    sig_sq = noise_sigma * noise_sigma
    input_scale = lax.rsqrt(sig_sq + 1.0)
    skip_scale = 1.0 / (sig_sq + 1.0)
    output_scale = noise_sigma * lax.rsqrt(sig_sq + 1.0)
    loss_scale = (sig_sq + 1.0) / sig_sq
    modulation = jnp.dot(noise_feat[None, :], w_cond, precision=highest)[0]
    scale_one, shift_one, scale_two, shift_two = jnp.split(modulation, 4)
    noisy = target + noise_sigma * noise_eps
    node_local = pix_node - block_start
    pixel_in = jnp.concatenate([prev_state, input_scale * noisy], 1).astype(jnp.bfloat16)
    node_in = jax.ops.segment_sum(pixel_in.astype(jnp.float32), node_local, node_rows)
    h_zero = jnp.dot(node_in, w_enc.astype(jnp.bfloat16).astype(jnp.float32), precision=highest)
    valid_mask = (node_local < valid_count[0]).astype(jnp.float32)[:, None]
    residual = target - prev_state
    stat_sum, count_sum = lax.psum(
        (jnp.sum(valid_mask * residual * residual, 0), jnp.sum(valid_mask)), "node"
    )
    var_weight = 1.0 / (stat_sum / count_sum + norm_eps)
    loss_count = count_sum * VARS
    normed_zero, inv_zero = standardize(h_zero)
    norm_one = (normed_zero * (1 + scale_one) + shift_one).astype(jnp.bfloat16)
    qkv_low = (
        jnp.dot(norm_one, w_qkv, preferred_element_type=jnp.float32)
        .reshape(node_rows, heads_here, 3, HD)
        .astype(jnp.bfloat16)
    )
    query_low = qkv_low[:, :, 0]
    keyval = qkv_low[:, :, 1:].reshape(node_rows, heads_here * 2 * HD)
    source = extended(keyval, (("node", 0),), node_rows)
    row_index = (neighbours - block_start + node_rows) % (node_rows * groups)
    near_rows = source[row_index].reshape(node_rows, NBR, heads_here, 2, HD)
    key_near = near_rows[:, :, :, 0]
    value_near = near_rows[:, :, :, 1]
    score_scale = 1.0 / math.sqrt(HD)
    scores = (
        jnp.einsum("nhe,njhe->nhj", query_low, key_near, preferred_element_type=jnp.float32)
        * score_scale
    )
    live_mask = jnp.arange(NBR)[None, None, :] < nbr_count[:, None, None]
    attn_probs = jax.nn.softmax(jnp.where(live_mask, scores, -1e30), axis=-1)
    probs_low = attn_probs.astype(jnp.bfloat16)
    mixed_low = (
        jnp.einsum("nhj,njhe->nhe", probs_low, value_near, preferred_element_type=jnp.float32)
        .astype(jnp.bfloat16)
        .reshape(node_rows, heads_here * HD)
    )
    h_one = h_zero + lax.psum(contract(mixed_low, w_out, 1, 1), "head")
    normed_one, inv_one = standardize(h_one)
    norm_two = (normed_one * (1 + scale_two) + shift_two).astype(jnp.bfloat16)
    up_proj = jnp.dot(norm_two, w_up, preferred_element_type=jnp.float32)
    act_low = jax.nn.silu(up_proj).astype(jnp.bfloat16)
    h_two = h_one + lax.psum(contract(act_low, w_down, 1, 1), "head")
    normed_two, inv_two = standardize(h_two)
    final_low = normed_two.astype(jnp.bfloat16)
    w_dec_low = w_dec.astype(jnp.bfloat16)
    decoded = jnp.dot(final_low, w_dec_low, preferred_element_type=jnp.float32)
    read_local = pix_read - block_start
    pixel_field = (
        decoded[read_local[:, 0]] + decoded[read_local[:, 1]] + decoded[read_local[:, 2]]
    ) / 3.0
    pixel_error = skip_scale * noisy + output_scale * pixel_field - target
    weighted = valid_mask * loss_scale * var_weight
    loss_part = jnp.sum(weighted * pixel_error * pixel_error)
    d_field = output_scale * (2.0 / loss_count) * weighted * pixel_error
    d_decoded = jax.ops.segment_sum(
        jnp.repeat(d_field / 3.0, 3, axis=0), read_local.reshape(-1), node_rows
    )
    d_dec_low = d_decoded.astype(jnp.bfloat16)
    grad_dec = contract(final_low, d_dec_low, 0, 0)
    d_two = norm_back(normed_two, inv_two, contract(d_dec_low, w_dec_low, 1, 1))
    d_two_low = d_two.astype(jnp.bfloat16)
    grad_down = contract(d_two_low, act_low, 0, 0)
    d_act = jnp.dot(d_two_low, w_down, preferred_element_type=jnp.float32)
    gating = jax.nn.sigmoid(up_proj)
    d_up_low = (d_act * gating * (1 + up_proj * (1 - gating))).astype(jnp.bfloat16)
    grad_up = contract(norm_two, d_up_low, 0, 0)
    d_mid = lax.psum(contract(d_up_low, w_up, 1, 1), "head")
    grad_scale_two = jnp.sum(d_mid * normed_one, 0)
    grad_shift_two = jnp.sum(d_mid, 0)
    d_one = d_two + norm_back(normed_one, inv_one, d_mid * (1 + scale_two))
    d_one_low = d_one.astype(jnp.bfloat16)
    grad_out = contract(d_one_low, mixed_low, 0, 0)
    d_mixed = (
        jnp.dot(d_one_low, w_out, preferred_element_type=jnp.float32)
        .astype(jnp.bfloat16)
        .reshape(node_rows, heads_here, HD)
    )
    d_probs = jnp.einsum("nhe,njhe->nhj", d_mixed, value_near, preferred_element_type=jnp.float32)
    d_value = jnp.einsum("nhj,nhe->njhe", probs_low, d_mixed, preferred_element_type=jnp.float32)
    d_scores = (
        attn_probs * (d_probs - jnp.sum(attn_probs * d_probs, -1, keepdims=True)) * score_scale
    )
    d_query = jnp.einsum("nhj,njhe->nhe", d_scores, key_near, preferred_element_type=jnp.float32)
    d_key = jnp.einsum("nhj,nhe->njhe", d_scores, query_low, preferred_element_type=jnp.float32)
    d_near = jnp.stack([d_key, d_value], 3).reshape(node_rows * NBR, heads_here * 2 * HD)
    d_source = jax.ops.segment_sum(d_near, row_index.reshape(-1), source.shape[0])
    from_above = passed_along(d_source[:node_rows], "node", -1)
    from_below = passed_along(d_source[2 * node_rows :], "node", 1)
    d_keyval = d_source[node_rows : 2 * node_rows] + from_above + from_below
    d_kv = d_keyval.reshape(node_rows, heads_here, 2, HD)
    d_qkv_low = (
        jnp.concatenate([d_query[:, :, None], d_kv], 2)
        .astype(jnp.bfloat16)
        .reshape(node_rows, heads_here * 3 * HD)
    )
    grad_qkv = contract(norm_one, d_qkv_low, 0, 0)
    d_norm = lax.psum(contract(d_qkv_low, w_qkv, 1, 1), "head")
    grad_scale_one = jnp.sum(d_norm * normed_zero, 0)
    grad_shift_one = jnp.sum(d_norm, 0)
    d_zero = d_one + norm_back(normed_zero, inv_zero, d_norm * (1 + scale_one))
    grad_enc = lax.dot_general(node_in, d_zero, (((0,), (0,)), ((), ())), precision=highest)
    d_modulation = jnp.concatenate([grad_scale_one, grad_shift_one, grad_scale_two, grad_shift_two])
    grad_cond = noise_feat[:, None] * d_modulation[None, :]
    grad_attn = jnp.concatenate(
        [
            grad_qkv.reshape(model_width, heads_here, 3, HD),
            grad_out.reshape(model_width, heads_here, 1, HD),
        ],
        2,
    ).reshape(model_width, block_cols)
    grad_layer = jnp.stack([grad_attn, grad_up, grad_down])
    layer_share = lax.psum_scatter(grad_layer, "node", scatter_dimension=1, tiled=True)
    grad_enc, grad_cond, grad_dec = lax.psum((grad_enc, grad_cond, grad_dec), "node")
    small_sq = (
        jnp.sum(grad_enc * grad_enc) + jnp.sum(grad_cond * grad_cond) + jnp.sum(grad_dec * grad_dec)
    )
    layer_sq = jnp.sum(layer_share * layer_share)
    loss_term = loss_part * (lax.axis_index("head") == 0).astype(jnp.float32)
    total_sq, loss_sum = lax.psum((layer_sq, loss_term), ("head", "node"))
    grad_norm = jnp.sqrt(total_sq + small_sq)
    clip_factor = clip_limit / jnp.maximum(grad_norm, clip_limit)
    clipped = clip_factor * layer_share
    stat_new = lax.psum(jnp.einsum("idb,idc->ibc", clipped, clipped, precision=highest), "node")
    basis_old = soap_basis[:, 0]
    rotated = jnp.einsum("idb,ibc->idc", clipped, basis_old, precision=highest)
    first_new = beta_first * soap_first + (1 - beta_first) * rotated
    second_new = beta_second * soap_second + (1 - beta_second) * rotated * rotated
    direction = (
        first_new
        / (1 - beta_first**STEP)
        / (jnp.sqrt(second_new / (1 - beta_second**STEP)) + adam_epsilon)
    )
    step_back = jnp.einsum("idc,ibc->idb", direction, basis_old, precision=highest)
    layer_new = layer_w - rate_layer * (step_back + decay_rate * layer_w)
    stats_new = beta_stats * soap_stats[:, 0] + (1 - beta_stats) * stat_new
    product = jnp.einsum("ibc,icd->ibd", stats_new, basis_old, precision=highest)
    gram_matrix = jnp.einsum("ibc,ibd->icd", product, product, precision=highest)
    chol_lower = jnp.linalg.cholesky(gram_matrix)
    basis_new = jnp.swapaxes(
        lax.linalg.triangular_solve(
            chol_lower, jnp.swapaxes(product, 1, 2), left_side=True, lower=True
        ),
        1,
        2,
    )
    enc_new = adam_small(w_enc, clip_factor * grad_enc, enc_first, enc_second)
    cond_new = adam_small(w_cond, clip_factor * grad_cond, cond_first, cond_second)
    dec_new = adam_small(w_dec, clip_factor * grad_dec, dec_first, dec_second)
    return (
        jnp.reshape(loss_sum, (1,)),
        jnp.reshape(loss_count, (1,)),
        jnp.reshape(grad_norm, (1,)),
        layer_new,
        first_new,
        second_new,
        basis_new[:, None],
        stats_new[:, None],
        enc_new[0],
        enc_new[1],
        enc_new[2],
        cond_new[0],
        cond_new[1],
        cond_new[2],
        dec_new[0],
        dec_new[1],
        dec_new[2],
    )


def solution(mesh):
    placed = (
        P("node", None),
        P("node", None),
        P("node", None),
        P(),
        P("node"),
        P("node", None),
        P("node"),
        P("node"),
        P("node", None),
        P(),
        P(),
        P(),
        P(None, "node", "head"),
        P(None, "node", "head"),
        P(None, "node", "head"),
        P(None, "head", None, None),
        P(None, "head", None, None),
        P(),
        P(),
        P(),
        P(),
        P(),
        P(),
    )
    return jax.shard_map(
        local,
        mesh=mesh,
        in_specs=placed,
        out_specs=(
            P(),
            P(),
            P(),
            P(None, "node", "head"),
            P(None, "node", "head"),
            P(None, "node", "head"),
            P(None, "head", None, None),
            P(None, "head", None, None),
            P(),
            P(),
            P(),
            P(),
            P(),
            P(),
            P(),
            P(),
            P(),
        ),
        check_vma=False,
    )
```

profile of v0, /device:TPU:0, one launch (start us, length us, event | category | flops | bytes accessed | tf_op | source)
XLA Modules:
  0.0 2269.5 jit_solution(7960003568067507774)
XLA Ops:
  41.5 67.7 %scatter_custom_fusion = f32[2048,168]{1,0:T(8,128)} fusion(s32[12288]{0:T(1024)S(1)} %get-tuple-element.171, f32[12288,168]{1,0:T(8,128)} %copy.288, f32[]{:T(128)} %constant.272.clone.1), kind=kCustom, calls=%fused_computation.132 | custom fusion | flops 2064384 | bytes 1376768 | tf_op jit(solution)/shard_map/scatter-add | solution.py:135
  161.7 123.0 %gather_fusion = bf16[32768,256]{1,0:T(8,128)(2,1)} fusion(bf16[6144,256]{1,0:T(8,128)(2,1)} %pad_maximum_fusion.1, s32[32768]{0:T(1024)S(1)} %broadcast_clamp_fusion), kind=kCustom, calls=%fused_computation | custom fusion | bytes 33685504 | tf_op jit(solution)/shard_map/gather | solution.py:155
  308.4 32.7 %fusion.163 = (bf16[2048,16,1,1,128]{4,3,1,0,2:T(2,128)(2,1)}, bf16[2048,16,1,1,128]{4,3,1,0,2:T(2,128)(2,1)}) fusion(bf16[2048,16,1,2,128]{4,3,1,0,2:T(2,128)(2,1)} %reshape.316), kind=kLoop, calls=%fused_computation.294 | loop fusion | bytes 33554432 | tf_op jit(solution)/shard_map/slice | solution.py:156
  401.9 75.7 %all-reduce.11.cloned.1.call-done = f32[2048,512]{0,1:T(8,128)} async-done(((f32[2048,512]{0,1:T(8,128)}), f32[2048,512]{0,1:T(8,128)}) %all-reduce.11.cloned.1.call-update) | async-done | bytes 4194320 | tf_op jit(solution)/shard_map/psum | solution.py:171
  493.0 102.9 %all-reduce.13.cloned.1.call-done = f32[2048,512]{0,1:T(8,128)} async-done(((f32[2048,512]{0,1:T(8,128)}), f32[2048,512]{0,1:T(8,128)}) %all-reduce.13.cloned.1.call-update) | async-done | bytes 4194320 | tf_op jit(solution)/shard_map/psum | solution.py:176
  604.0 42.2 %gather_fusion.3 = f32[12288,84]{1,0:T(8,128)} fusion(f32[2048,84]{1,0:T(8,128)} %fusion.90, s32[12288]{0:T(1024)S(1)} %broadcast_clamp_fusion.1), kind=kCustom, calls=%fused_computation.3 | custom fusion | bytes 8306688 | tf_op jit(solution)/shard_map/gather | solution.py:183
  652.4 42.2 %gather_fusion.1 = f32[12288,84]{1,0:T(8,128)} fusion(f32[2048,84]{1,0:T(8,128)} %fusion.90, s32[12288]{0:T(1024)S(1)} %broadcast_clamp_fusion.3), kind=kCustom, calls=%fused_computation.1 | custom fusion | bytes 8306688 | tf_op jit(solution)/shard_map/gather | solution.py:183
  700.7 42.2 %gather_fusion.2 = f32[12288,84]{1,0:T(8,128)} fusion(f32[2048,84]{1,0:T(8,128)} %fusion.90, s32[12288]{0:T(1024)S(1)} %broadcast_clamp_fusion.2), kind=kCustom, calls=%fused_computation.2 | custom fusion | bytes 8306688 | tf_op jit(solution)/shard_map/gather | solution.py:183
  810.2 197.0 %scatter_custom_fusion.1 = f32[2048,84]{1,0:T(8,128)} fusion(s32[36864]{0:T(1024)} %reshape.392, f32[36864,84]{1,0:T(8,128)} %reshape.394, f32[]{:T(128)} %constant.272.clone.1), kind=kCustom, calls=%fused_computation.151 | custom fusion | flops 3096576 | bytes 688640 | tf_op jit(solution)/shard_map/scatter-add | solution.py:189
  1027.2 97.5 %all-reduce.15.cloned.1.call-done = f32[2048,512]{0,1:T(8,128)} async-done(((f32[2048,512]{0,1:T(8,128)}), f32[2048,512]{0,1:T(8,128)}) %all-reduce.15.cloned.1.call-update) | async-done | bytes 4194320 | tf_op jit(solution)/shard_map/psum | solution.py:201
  1178.6 33.5 %pad_maximum_fusion = f32[2048,16,1,2,128]{4,3,1,0,2:T(2,128)} fusion(f32[2048,16,1,1,128]{4,3,1,0,2:T(1,128)S(1)} %bitcast.221, f32[2048,16,1,1,128]{4,3,1,0,2:T(1,128)} %bitcast.222), kind=kLoop, calls=%fused_computation.12 | loop fusion | flops 8388608 | bytes 67108864 | tf_op jit(solution)/shard_map/stack | solution.py:219
  1212.1 186.8 %scatter_custom_fusion.2 = f32[6144,256]{1,0:T(8,128)} fusion(s32[32768]{0:T(1024)S(1)} %reshape.400, f32[4096,8,2,128]{3,2,1,0:T(2,128)} %bitcast.220, f32[]{:T(128)} %constant.272.clone.1), kind=kCustom, calls=%fused_computation.9 | custom fusion | flops 8388608 | bytes 39845892 | tf_op jit(solution)/shard_map/scatter-add | solution.py:220
  1418.0 33.0 %collective-permute-done.3 = f32[2048,256]{1,0:T(8,128)S(1)} collective-permute-done((f32[2048,256]{1,0:T(8,128)}, f32[2048,256]{1,0:T(8,128)S(1)}, u32[]{:S(2)}, u32[]{:S(2)}) %collective-permute-start.3) | collective-permute-done | bytes 2097184 | tf_op jit(solution)/shard_map/ppermute | solution.py:44
  1494.9 71.8 %all-reduce.17.cloned.1.call-done = f32[2048,512]{0,1:T(8,128)} async-done(((f32[2048,512]{0,1:T(8,128)}), f32[2048,512]{0,1:T(8,128)}) %all-reduce.17.cloned.1.call-update) | async-done | bytes 4194320 | tf_op jit(solution)/shard_map/psum | solution.py:231
  1602.3 39.9 %all-reduce.21.cloned.1.call-done = (f32[168,512]{1,0:T(8,128)}, f32[32,2048]{1,0:T(8,128)}, f32[512,84]{0,1:T(8,128)}) async-done(((f32[168,512]{1,0:T(8,128)}, f32[32,2048]{1,0:T(8,128)}, f32[512,84]{0,1:T(8,128)}), (f32[168,512]{1,0:T(8,128)}, f32[32,2048]{1,0:T(8,128)}, f32[512,84]{0,1:T(8,128)})) %all-reduce.21.cloned.1.call-update) | async-done | bytes 778256 | tf_op jit(solution)/shard_map/psum | solution.py:247
  1649.0 35.5 %reduce-scatter.2.cloned.1.call-done = f32[3,64,512]{2,1,0:T(8,128)} async-done(((f32[3,512,512]{2,1,0:T(8,128)}), f32[3,64,512]{2,1,0:T(8,128)}) %reduce-scatter.2.cloned.1.call-update) | async-done | bytes 393232 | tf_op jit(solution)/shard_map/reduce_scatter | solution.py:246
  1686.2 39.0 %all-reduce.1 = (f32[1]{0:T(128)}, f32[]{:T(128)}) all-reduce(f32[1]{0:T(128)} %bitcast.27, f32[]{:T(128)} %multiply_reduce_fusion.11), channel_id=1, replica_groups=mesh['head'=4,'node'=8] {'head','node'}, use_global_device_ids=true, to_apply=%region_16.17 | all-reduce | flops 2 | bytes 16 | tf_op jit(solution)/shard_map/psum | solution.py:253
  1744.3 64.9 %all-reduce.19.cloned.1.call-done = f32[3,512,512]{2,1,0:T(8,128)} async-done(((f32[3,512,512]{2,1,0:T(8,128)}), f32[3,512,512]{2,1,0:T(8,128)}) %all-reduce.19.cloned.1.call-update) | async-done | bytes 3145744 | tf_op jit(solution)/shard_map/psum | solution.py:257
  1834.6 35.2 %custom-call.34 = f32[3,128,128]{2,1,0:T(8,128)S(1)} custom-call(f32[3,128,128]{2,1,0:T(8,128)S(1)} %cholesky.274), custom_call_target="Cholesky" | custom-call | tf_op jit(solution)/shard_map/jit(cholesky)/cholesky | solution.py:272
  1907.9 36.0 %custom-call.36 = f32[3,128,128]{2,1,0:T(8,128)S(1)} custom-call(f32[3,128,128]{2,1,0:T(8,128)} %cholesky.278), custom_call_target="Cholesky" | custom-call | tf_op jit(solution)/shard_map/jit(cholesky)/cholesky | solution.py:272
  1944.7 30.9 %custom-call.37 = f32[3,1,128,128]{2,3,1,0:T(8,128)} custom-call(f32[3,1,128,128]{3,2,1,0:T(8,128)} %get-tuple-element.196), custom_call_target="InvertDiagBlocksLowerTriangular" | custom-call | tf_op jit(solution)/shard_map/jit(cholesky)/cholesky | solution.py:272
  1981.6 37.1 %custom-call.38 = f32[3,128,128]{2,1,0:T(8,128)} custom-call(f32[3,128,128]{2,1,0:T(8,128)} %cholesky.283), custom_call_target="Cholesky" | custom-call | tf_op jit(solution)/shard_map/jit(cholesky)/cholesky | solution.py:272
  2056.1 36.6 %custom-call.40 = f32[3,128,128]{2,1,0:T(8,128)} custom-call(f32[3,128,128]{2,1,0:T(8,128)} %convolution_subtract_fusion.3), custom_call_target="Cholesky" | custom-call | tf_op jit(solution)/shard_map/jit(cholesky)/cholesky | solution.py:272
  2113.4 119.5 %custom-call.41 = f32[3,4,128,128]{2,3,1,0:T(8,128)} custom-call(f32[3,4,128,128]{3,2,1,0:T(8,128)} %bitcast.248), custom_call_target="InvertDiagBlocksLowerTriangular" | custom-call | tf_op jit(solution)/shard_map/triangular_solve | solution.py:274
  (327 shorter events, 637.8 us)
Async XLA Ops:
  7.2 1728.8 %copy-start = (f32[3,1,512,512]{3,2,1,0:T(8,128)S(1)}, f32[3,1,512,512]{3,2,1,0:T(8,128)}, u32[]{:S(2)}) copy-start(f32[3,1,512,512]{3,2,1,0:T(8,128)} %param.38) | copy-start | bytes 9437188
  7.2 110.2 %all-gather.2.cloned.1.call-start = ((), (), s32[]{:S(2)}) async-start(), calls=%async_computation.1 | async-start | bytes 1769472 | tf_op jit(solution)/shard_map/all_gather | solution.py:116
  9.1 468.4 %all-reduce.11.cloned.1.call-start = ((), (), s32[]{:S(2)}) async-start(), calls=%async_computation.2 | async-start | bytes 8388608 | tf_op jit(solution)/shard_map/psum | solution.py:171
  35.4 75.8 %copy-start.41 = (f32[168,512]{1,0:T(8,128)S(1)}, f32[168,512]{1,0:T(8,128)}, u32[]{:S(2)}) copy-start(f32[168,512]{1,0:T(8,128)} %param.32) | copy-start | bytes 1032196
  129.2 26.5 %collective-permute-start.1 = (bf16[2048,256]{1,0:T(8,128)(2,1)}, bf16[2048,256]{1,0:T(8,128)(2,1)}, u32[]{:S(2)}, u32[]{:S(2)}) collective-permute-start(bf16[2048,256]{1,0:T(8,128)(2,1)} %copy.293), channel_id=1, source_target_pairs={{1,0},{2,1},{3,2},{4,3},{5,4},{6,5},{7,6},{0,7},{9,8},{10,9},{11,1... | collective-permute-start | bytes 3145736 | tf_op jit(solution)/shard_map/ppermute | solution.py:37
  133.7 24.9 %collective-permute-start = (bf16[2048,256]{1,0:T(8,128)(2,1)}, bf16[2048,256]{1,0:T(8,128)(2,1)}, u32[]{:S(2)}, u32[]{:S(2)}) collective-permute-start(bf16[2048,256]{1,0:T(8,128)(2,1)} %copy.293), channel_id=1, source_target_pairs={{0,1},{1,2},{2,3},{3,4},{4,5},{5,6},{6,7},{7,0},{8,9},{9,10},{10,1... | collective-permute-start | bytes 3145736 | tf_op jit(solution)/shard_map/ppermute | solution.py:34
  341.2 11.5 copy-start.53
  370.6 20.7 copy-start.50
  374.3 221.5 %all-reduce.13.cloned.1.call-start = ((), (), s32[]{:S(2)}) async-start(), calls=%async_computation.3 | async-start | bytes 8388608 | tf_op jit(solution)/shard_map/psum | solution.py:176
  491.8 632.9 %all-reduce.15.cloned.1.call-start = ((), (), s32[]{:S(2)}) async-start(), calls=%async_computation.4 | async-start | bytes 8388608 | tf_op jit(solution)/shard_map/psum | solution.py:201
  1020.7 546.0 %all-reduce.17.cloned.1.call-start = ((), (), s32[]{:S(2)}) async-start(), calls=%async_computation.6 | async-start | bytes 8388608 | tf_op jit(solution)/shard_map/psum | solution.py:231
  1402.7 48.3 %collective-permute-start.3 = (f32[2048,256]{1,0:T(8,128)}, f32[2048,256]{1,0:T(8,128)S(1)}, u32[]{:S(2)}, u32[]{:S(2)}) collective-permute-start(f32[2048,256]{1,0:T(8,128)} %get-tuple-element.183), channel_id=1, source_target_pairs={{0,1},{1,2},{2,3},{3,4},{4,5},{5,6},{6,7},{7,0},{8,9},{9,10},{10,1... | collective-permute-start | bytes 6291464 | tf_op jit(solution)/shard_map/ppermute | solution.py:44
  1402.7 48.3 %collective-permute-start.2 = (f32[2048,256]{1,0:T(8,128)S(1)}, f32[2048,256]{1,0:T(8,128)S(1)}, u32[]{:S(2)}, u32[]{:S(2)}) collective-permute-start(f32[2048,256]{1,0:T(8,128)S(1)} %get-tuple-element.182), channel_id=1, source_target_pairs={{0,7},{1,0},{2,1},{3,2},{4,3},{5,4},{6,5},{7,6},{8,15},{9,8},{10,9... | collective-permute-start | bytes 6291464 | tf_op jit(solution)/shard_map/ppermute | solution.py:44
  1463.3 178.8 %all-reduce.21.cloned.1.call-start = ((), (), s32[]{:S(2)}) async-start(), calls=%async_computation.8 | async-start | bytes 1572864 | tf_op jit(solution)/shard_map/psum | solution.py:247
  1472.0 11.3 copy-start.8
  1472.0 11.3 copy-start.28
  1486.3 80.4 %copy-start.52 = (f32[2048]{0:T(1024)S(1)}, f32[2048]{0:T(1024)}, u32[]{:S(2)}) copy-start(f32[2048]{0:T(1024)} %copy-done.51) | copy-start | bytes 24580
  1486.3 80.4 %copy-start.55 = (f32[2048]{0:T(1024)S(1)}, f32[2048]{0:T(1024)}, u32[]{:S(2)}) copy-start(f32[2048]{0:T(1024)} %copy-done.54) | copy-start | bytes 24580
  1486.3 80.4 %copy-start.57 = (f32[512]{0:T(512)S(1)}, f32[512]{0:T(512)}, u32[]{:S(2)}) copy-start(f32[512]{0:T(512)} %copy-done.56) | copy-start | bytes 6148
  1494.9 77.2 %copy-start.60 = (f32[32]{0:T(128)S(1)}, f32[32]{0:T(128)}, u32[]{:S(2)}) copy-start(f32[32]{0:T(128)} %copy-done.59) | copy-start | bytes 388
  1572.9 11.4 copy-start.62
  1584.2 100.2 %reduce-scatter.2.cloned.1.call-start = ((), (), s32[]{:S(2)}) async-start(), calls=%async_computation.5 | async-start | bytes 3538944 | tf_op jit(solution)/shard_map/reduce_scatter | solution.py:246
  1595.6 213.6 %all-reduce.19.cloned.1.call-start = ((), (), s32[]{:S(2)}) async-start(), calls=%async_computation.7 | async-start | bytes 6291456 | tf_op jit(solution)/shard_map/psum | solution.py:257
  2053.3 45.9 %copy-start.64 = (s32[4]{0:T(128)S(1)}, s32[4]{0:T(128)}, u32[]{:S(2)}) copy-start(s32[4]{0:T(128)} %iota_multiply_fusion) | copy-start | bytes 52
  (53 other events, 236.1 us)
Sparse Core Ops, SparseCore 0:
  10.2 27.7 all-gather.1
  374.4 103.0 all-reduce.10
  492.0 103.8 all-reduce.12
  1020.9 103.8 all-reduce.14
  1463.5 103.1 all-reduce.16
  1584.4 57.7 all-reduce.20
  1645.1 39.3 reduce-scatter.1
  1731.5 77.5 all-reduce.18
where the time goes:
time: 2280 us; the launch traced here: 2270 us
  other arithmetic  994 us (44%)
  waiting for transfers between devices  540 us (24%)
  local copies, waits for them, and re-layouts  488 us (21%)
  matrix products  160 us (7%)
  blocking collectives  54.6 us (2%)
  between operations  23.1 us (1%)
    another operation x18, other arithmetic, local(): chol_lower = jnp.linalg.cholesky(gram_matrix)  242 us
    scatter-add x1, other arithmetic, local(): jax.ops.segment_sum(jnp.repeat(d_field / 3.0, 3, axis=0), read_local.resh...  197 us
    scatter-add x1, other arithmetic, local(): jax.ops.segment_sum(d_near, row_index.reshape(-1), source.shape[0])  187 us
    another operation x4, other arithmetic, local(): lax.linalg.triangular_solve(chol_lower, jnp.swapaxes(product, 1, 2), left...  125 us
    gather x1, local copies, waits for them, and re-layouts, local(): near_rows = source[row_index].reshape(node_rows, NBR, heads_here, 2, HD)  123 us
    psum x1, waiting for transfers between devices, local(): h_two = h_one + lax.psum(contract(act_low, w_down, 1, 1), 'head')  103 us
    psum x1, waiting for transfers between devices, local(): d_mid = lax.psum(contract(d_up_low, w_up, 1, 1), 'head')  97.5 us
    psum x1, waiting for transfers between devices, local(): h_one = h_zero + lax.psum(contract(mixed_low, w_out, 1, 1), 'head')  75.7 us
  transfers between devices with their start and end apart: 12, of which 10 were waited for; matrix products, arithmetic and copies ran while one was open for 9% of the time, Pallas kernels for 0%

commit v1 on v0

v1 whole, which is shorter than its diff:
```python
import functools
import math

import jax
import jax.numpy as jnp
from jax import lax
from jax.experimental import pallas as pl
from jax.experimental.pallas import tpu as pltpu
from jax.sharding import PartitionSpec as P

HD = 128
VARS = 84
NF = 32
NBR = 16
LEVELS = 1000
STEP = 10

SLOT = 128
SLIM = 96
GROUP = 256 // NBR
BLOCK = 128

highest = lax.Precision.HIGHEST
clip_limit = 0.01
beta_first = 0.9
beta_second = 0.95
beta_stats = 0.95
adam_epsilon = 1e-08
rate_layer = 0.02
rate_small = 0.05
decay_rate = 0.1
norm_eps = 1e-05

f32 = jnp.float32
bf16 = jnp.bfloat16
MIB = 2**20


def passed_along(x, axis, by):
    length = lax.axis_size(axis)
    return lax.ppermute(x, axis, [(i, (i + by) % length) for i in range(length)])


def noise_terms(noise_level):
    level_frac = noise_level[0].astype(f32) / (LEVELS - 1)
    noise_sigma = 0.05 * jnp.exp(level_frac * math.log(40.0))
    frequency = 1.0 + jnp.arange(NF // 2).astype(f32)
    phase_angle = jnp.log(noise_sigma) * frequency
    return (noise_sigma, jnp.concatenate([jnp.sin(phase_angle), jnp.cos(phase_angle)]))


def standardize(values_in):
    row_mean = jnp.mean(values_in, -1, keepdims=True)
    centered = values_in - row_mean
    inv_std = lax.rsqrt(jnp.mean(centered * centered, -1, keepdims=True) + norm_eps)
    return (centered * inv_std, inv_std)


def norm_back(normed, inv_std, grad_in):
    return inv_std * (
        grad_in
        - jnp.mean(grad_in, -1, keepdims=True)
        - normed * jnp.mean(grad_in * normed, -1, keepdims=True)
    )


def contract(left, right, left_dim, right_dim, precision=None):
    return lax.dot_general(
        left,
        right,
        (((left_dim,), (right_dim,)), ((), ())),
        preferred_element_type=f32,
        precision=precision,
    )


def halves(x):
    high = x.astype(bf16)
    return high, (x - high.astype(f32)).astype(bf16)


def thirds(x):
    high = x.astype(bf16)
    rest = x - high.astype(f32)
    return (high, *halves(rest))


def fold_lanes(x, op=jnp.add):
    parts = [x[:, i : i + 128] for i in range(0, x.shape[1], 128)]
    while len(parts) > 1:
        parts = [op(*parts[i : i + 2]) if i + 1 < len(parts) else parts[i] for i in range(0, len(parts), 2)]
    return parts[0]


def adam_small(weight, grad_item, first, second):
    first_new = beta_first * first + (1 - beta_first) * grad_item
    second_new = beta_second * second + (1 - beta_second) * grad_item * grad_item
    ratio = (
        first_new
        / (1 - beta_first**STEP)
        / (jnp.sqrt(second_new / (1 - beta_second**STEP)) + adam_epsilon)
    )
    return (weight - rate_small * (ratio + decay_rate * weight), first_new, second_new)


def smem():
    return pl.BlockSpec(memory_space=pltpu.SMEM)


def whole(shape):
    zeros = (0,) * len(shape)
    return pl.BlockSpec(tuple(shape), lambda *_: zeros)


def params(mib=48):
    return pltpu.CompilerParams(vmem_limit_bytes=mib * MIB)


def encode_kernel(place_ref, scale_ref, node_ref, prev_ref, target_ref, eps_ref, in_ref, stat_ref, pix):
    step = pl.program_id(0)
    rows = in_ref.shape[0]
    tile = node_ref.shape[1]

    @pl.when(step == 0)
    def _():
        pix[...] = jnp.zeros_like(pix)
        in_ref[...] = jnp.zeros_like(in_ref)
        stat_ref[...] = jnp.zeros_like(stat_ref)

    prev = prev_ref[...]
    target = target_ref[...]
    noisy = target + scale_ref[0] * eps_ref[...]
    pix[:VARS] = prev.astype(bf16)
    pix[SLOT : SLOT + VARS] = (scale_ref[1] * noisy).astype(bf16)
    node = node_ref[...] - place_ref[0]
    mine = node - place_ref[1]
    spot = lax.broadcasted_iota(jnp.int32, (rows, tile), 0)
    onehot = (spot == mine).astype(f32).astype(bf16)
    in_ref[...] += contract(onehot, pix[...], 1, 1)
    valid = (node < place_ref[2]).astype(f32)
    residual = target - prev
    stat_ref[:VARS] += fold_lanes(valid * residual * residual)
    stat_ref[SLIM - 1 : SLIM] += fold_lanes(valid)


def encode(place, scales, node_row, prev, target, eps, rows, tile):
    pixels = prev.shape[1]
    pixel_block = pl.BlockSpec((VARS, tile), lambda i: (0, i))
    return pl.pallas_call(
        encode_kernel,
        grid=(pixels // tile,),
        in_specs=[smem(), smem(), pl.BlockSpec((1, tile), lambda i: (0, i))] + [pixel_block] * 3,
        out_specs=[whole((rows, 2 * SLOT)), whole((SLIM, 128))],
        out_shape=[
            jax.ShapeDtypeStruct((rows, 2 * SLOT), f32),
            jax.ShapeDtypeStruct((SLIM, 128), f32),
        ],
        scratch_shapes=[pltpu.VMEM((2 * SLOT, tile), bf16)],
        compiler_params=params(),
        name="encode",
    )(place, scales, node_row, prev, target, eps)


def enter_kernel(in_ref, w_ref, mod_ref, zero_ref, norm_ref):
    w = w_ref[...]
    h_zero = sum(contract(part, w, 1, 0) for part in thirds(in_ref[...]))
    zero_ref[...] = h_zero
    normed, _ = standardize(h_zero)
    norm_ref[...] = (normed * (1 + mod_ref[0:1]) + mod_ref[1:2]).astype(bf16)


def enter(node_in, w_enc, modulation):
    rows, width = node_in.shape[0], w_enc.shape[1]
    return pl.pallas_call(
        enter_kernel,
        out_shape=[
            jax.ShapeDtypeStruct((rows, width), f32),
            jax.ShapeDtypeStruct((rows, width), bf16),
        ],
        compiler_params=params(),
        name="enter",
    )(node_in, w_enc, modulation)


def project_kernel(norm_ref, w_ref, q_ref, kv_ref):
    out = contract(norm_ref[...], w_ref[...], 1, 0).astype(bf16)
    q_ref[...] = out[:, :HD]
    kv_ref[...] = out[:, HD : 3 * HD]


def project(norm_all, w_attn, tile):
    nodes, width = norm_all.shape
    return pl.pallas_call(
        project_kernel,
        grid=(nodes // tile,),
        in_specs=[
            pl.BlockSpec((tile, width), lambda i: (i, 0)),
            pl.BlockSpec((width, 3 * HD), lambda i: (0, 0)),
        ],
        out_specs=[
            pl.BlockSpec((tile, HD), lambda i: (i, 0)),
            pl.BlockSpec((tile, 2 * HD), lambda i: (i, 0)),
        ],
        out_shape=[
            jax.ShapeDtypeStruct((nodes, HD), bf16),
            jax.ShapeDtypeStruct((nodes, 2 * HD), bf16),
        ],
        compiler_params=params(),
        name="project",
    )(norm_all, w_attn)


def count_kernel(slot_ref, count_ref):
    groups = slot_ref.shape[0]
    bands = count_ref.shape[1] // 256
    lane = lax.broadcasted_iota(jnp.int32, (GROUP, 256), 1)
    sub = lax.broadcasted_iota(jnp.int32, (GROUP, 256), 0)
    own = lane // NBR == sub
    spot = lax.broadcasted_iota(jnp.int32, (256, 256), 0)
    for g in range(groups):
        row = slot_ref[g : g + 1]
        band = jnp.where(own, row >> 8, -1)
        left = jnp.concatenate([(band == t).astype(f32).astype(bf16) for t in range(bands)], 0)
        right = (spot == (row & 255)).astype(f32).astype(bf16)
        found = contract(left, right, 1, 1).astype(bf16)
        for t in range(bands):
            count_ref[g * GROUP : (g + 1) * GROUP, t * 256 : (t + 1) * 256] = found[
                t * GROUP : (t + 1) * GROUP
            ]


def count_slots(slots, reach, tile_groups):
    groups = slots.shape[0]
    return pl.pallas_call(
        count_kernel,
        grid=(groups // tile_groups,),
        in_specs=[pl.BlockSpec((tile_groups, 256), lambda i: (i, 0))],
        out_specs=pl.BlockSpec((tile_groups * GROUP, reach), lambda i: (i, 0)),
        out_shape=jax.ShapeDtypeStruct((groups * GROUP, reach), bf16),
        compiler_params=params(),
        name="count_slots",
    )(slots)


def attend_kernel(q_ref, below_ref, here_ref, above_ref, count_ref, e_ref, mix_ref, low_ref, s_scr, chunk):
    tile = q_ref.shape[0]
    nodes = here_ref.shape[0]
    q = q_ref[...]
    top = jnp.full((tile, 128), -1e30, f32)
    for b, kv_ref in enumerate((below_ref, here_ref, above_ref)):
        for at in range(0, nodes, chunk):
            cols = slice(b * nodes + at, b * nodes + at + chunk)
            s = contract(q, kv_ref[at : at + chunk, :HD], 1, 1)
            s = jnp.where(count_ref[:, cols].astype(f32) > 0, s, -1e30)
            s_scr[:, cols] = s
            top = jnp.maximum(top, fold_lanes(s, jnp.maximum))
    top = jnp.max(top, 1, keepdims=True)
    factor = math.log2(math.e) / math.sqrt(HD)
    total = jnp.zeros((tile, 128), f32)
    mixed = jnp.zeros((tile, HD), f32)
    for b, kv_ref in enumerate((below_ref, here_ref, above_ref)):
        for at in range(0, nodes, chunk):
            cols = slice(b * nodes + at, b * nodes + at + chunk)
            e = count_ref[:, cols].astype(f32) * jnp.exp2((s_scr[:, cols] - top) * factor)
            total += fold_lanes(e)
            e = e.astype(bf16)
            e_ref[:, cols] = e
            mixed += contract(e, kv_ref[at : at + chunk, HD:], 1, 0)
    inverse = 1.0 / jnp.sum(total, 1, keepdims=True)
    mixed = mixed * inverse
    mix_ref[:, :HD] = mixed
    mix_ref[:, HD:] = jnp.broadcast_to(inverse, (tile, HD))
    low_ref[...] = mixed.astype(bf16)


def attend(query, below, here, above, counts, tile, chunk):
    nodes, reach = counts.shape
    row = lambda width: pl.BlockSpec((tile, width), lambda i: (i, 0))
    return pl.pallas_call(
        functools.partial(attend_kernel, chunk=chunk),
        grid=(nodes // tile,),
        in_specs=[row(HD)] + [whole((nodes, 2 * HD))] * 3 + [row(reach)],
        out_specs=[row(reach), row(2 * HD), row(HD)],
        out_shape=[
            jax.ShapeDtypeStruct((nodes, reach), bf16),
            jax.ShapeDtypeStruct((nodes, 2 * HD), f32),
            jax.ShapeDtypeStruct((nodes, HD), bf16),
        ],
        scratch_shapes=[pltpu.VMEM((tile, reach), f32)],
        compiler_params=params(60),
        name="attend",
    )(query, below, here, above, counts)


def attend_back_kernel(
    q_ref, d_ref, mix_ref, e_ref, below_ref, here_ref, above_ref, dq_ref, low_ref, self_ref, high_ref, dk, dv, chunk
):
    step = pl.program_id(0)
    tile = q_ref.shape[0]
    nodes = here_ref.shape[0]

    @pl.when(step == 0)
    def _():
        dk[...] = jnp.zeros_like(dk)
        dv[...] = jnp.zeros_like(dv)

    grad = d_ref[...]
    wide = grad.astype(f32)
    inverse = mix_ref[:, HD : HD + 1]
    delta = jnp.sum(wide * mix_ref[:, :HD], 1, keepdims=True)
    gain = inverse * (1.0 / math.sqrt(HD))
    q_turned = q_ref[...].T
    d_turned = (wide * inverse).astype(bf16).T
    dq = jnp.zeros((tile, HD), f32)
    for b, kv_ref in enumerate((below_ref, here_ref, above_ref)):
        for at in range(0, nodes, chunk):
            cols = slice(b * nodes + at, b * nodes + at + chunk)
            key = kv_ref[at : at + chunk, :HD]
            dp = contract(grad, kv_ref[at : at + chunk, HD:], 1, 1)
            e = e_ref[:, cols]
            ds = (e.astype(f32) * ((dp - delta) * gain)).astype(bf16)
            dq += contract(ds, key, 1, 0)
            dk[:, cols] += contract(q_turned, ds, 1, 0)
            dv[:, cols] += contract(d_turned, e, 1, 0)
    dq_ref[...] = dq.astype(bf16)

    @pl.when(step == pl.num_programs(0) - 1)
    def _():
        for b, ref in enumerate((low_ref, self_ref, high_ref)):
            cols = slice(b * nodes, (b + 1) * nodes)
            ref[:HD] = dk[:, cols].astype(ref.dtype)
            ref[HD:] = dv[:, cols].astype(ref.dtype)


def attend_back(query, grad, mix, e, below, here, above, tile, chunk):
    nodes, reach = e.shape
    row = lambda width: pl.BlockSpec((tile, width), lambda i: (i, 0))
    return pl.pallas_call(
        functools.partial(attend_back_kernel, chunk=chunk),
        grid=(nodes // tile,),
        in_specs=[row(HD), row(HD), row(2 * HD), row(reach)] + [whole((nodes, 2 * HD))] * 3,
        out_specs=[row(HD)] + [whole((2 * HD, nodes))] * 3,
        out_shape=[
            jax.ShapeDtypeStruct((nodes, HD), bf16),
            jax.ShapeDtypeStruct((2 * HD, nodes), bf16),
            jax.ShapeDtypeStruct((2 * HD, nodes), f32),
            jax.ShapeDtypeStruct((2 * HD, nodes), bf16),
        ],
        scratch_shapes=[pltpu.VMEM((HD, reach), f32)] * 2,
        compiler_params=params(60),
        name="attend_back",
    )(query, grad, mix, e, below, here, above)


def forward_kernel(mixed_ref, zero_ref, w_ref, mod_ref, wdec_ref, one_ref, two_ref, norm_ref, up_ref, act_ref, dec_ref):
    heads, width = w_ref.shape[0], w_ref.shape[1]
    h_one = zero_ref[...] + sum(
        contract(mixed_ref[h], w_ref[h, :, 2 * width :], 1, 1) for h in range(heads)
    )
    one_ref[...] = h_one
    normed, _ = standardize(h_one)
    norm_two = (normed * (1 + mod_ref[2:3]) + mod_ref[3:4]).astype(bf16)
    norm_ref[...] = norm_two
    h_two = h_one
    for h in range(heads):
        up = contract(norm_two, w_ref[h, :, :width], 1, 0)
        up_ref[h] = up
        act = (up * jax.nn.sigmoid(up)).astype(bf16)
        act_ref[h] = act
        h_two = h_two + contract(act, w_ref[h, :, width : 2 * width], 1, 1)
    two_ref[...] = h_two
    final = standardize(h_two)[0].astype(bf16)
    high, low = halves(contract(wdec_ref[...], final, 1, 1))
    dec_ref[:SLIM] = high
    dec_ref[SLIM:] = low


def forward(mixed, h_zero, w_big, modulation, w_dec, tile):
    heads, rows = mixed.shape[:2]
    width = h_zero.shape[1]
    row = pl.BlockSpec((tile, width), lambda i: (i, 0))
    stack = lambda w: pl.BlockSpec((heads, tile, w), lambda i: (0, i, 0))
    return pl.pallas_call(
        forward_kernel,
        grid=(rows // tile,),
        in_specs=[stack(HD), row, whole(w_big.shape), whole(modulation.shape), whole(w_dec.shape)],
        out_specs=[row, row, row, stack(width), stack(width), pl.BlockSpec((2 * SLIM, tile), lambda i: (0, i))],
        out_shape=[
            jax.ShapeDtypeStruct((rows, width), f32),
            jax.ShapeDtypeStruct((rows, width), f32),
            jax.ShapeDtypeStruct((rows, width), bf16),
            jax.ShapeDtypeStruct((heads, rows, width), f32),
            jax.ShapeDtypeStruct((heads, rows, width), bf16),
            jax.ShapeDtypeStruct((2 * SLIM, rows), bf16),
        ],
        compiler_params=params(),
        name="forward",
    )(mixed, h_zero, w_big, modulation, w_dec)


def pixel_kernel(place_ref, scale_ref, node_ref, read_ref, target_ref, eps_ref, weight_ref, dec_ref, loss_ref, d_ref, hits, turned, total):
    step = pl.program_id(0)
    heads, _, rows = dec_ref.shape
    tile = target_ref.shape[1]

    @pl.when(step == 0)
    def _():
        turned[...] = jnp.zeros_like(turned)
        total[...] = jnp.zeros_like(total)
        loss_ref[...] = jnp.zeros_like(loss_ref)

    reads = read_ref[...] - place_ref[0]
    field = jnp.zeros((2 * SLIM, tile), f32)
    for h in range(heads):
        spot = lax.broadcasted_iota(jnp.int32, (rows, tile), 0) + h * rows
        hit = sum((spot == reads[k : k + 1]).astype(f32) for k in range(3)).astype(bf16)
        hits[h * rows : (h + 1) * rows] = hit
        field += contract(dec_ref[h], hit, 1, 0)
    field = (field[:VARS] + field[SLIM : SLIM + VARS]) / 3.0
    target = target_ref[...]
    noisy = target + scale_ref[0] * eps_ref[...]
    error = scale_ref[2] * noisy + scale_ref[3] * field - target
    valid = (node_ref[...] - place_ref[0] < place_ref[2]).astype(f32)
    weighted = valid * weight_ref[:, 0:1]
    loss_ref[:VARS] += fold_lanes(weighted * error * error)
    high, low = halves(scale_ref[4] * weighted * error)
    turned[:VARS] = high
    turned[SLOT : SLOT + VARS] = low
    total[...] += contract(hits[...], turned[...], 1, 1)

    @pl.when(step == pl.num_programs(0) - 1)
    def _():
        d_ref[...] = total[:, :SLOT] + total[:, SLOT:]


def pixels_back(place, scales, node_row, read_rows, target, eps, weight, decoded, tile):
    heads, _, rows = decoded.shape
    count = target.shape[1] // heads
    steps = count // tile
    at = lambda i, place: (0, place[3] * steps + i)
    fixed = lambda shape: pl.BlockSpec(tuple(shape), lambda i, place: (0,) * len(shape))
    return pl.pallas_call(
        pixel_kernel,
        grid_spec=pltpu.PrefetchScalarGridSpec(
            num_scalar_prefetch=1,
            grid=(steps,),
            in_specs=[
                smem(),
                pl.BlockSpec((1, tile), at),
                pl.BlockSpec((3, tile), at),
                pl.BlockSpec((VARS, tile), at),
                pl.BlockSpec((VARS, tile), at),
                fixed(weight.shape),
                fixed(decoded.shape),
            ],
            out_specs=[fixed((SLIM, 128)), fixed((heads * rows, SLOT))],
            scratch_shapes=[
                pltpu.VMEM((heads * rows, tile), bf16),
                pltpu.VMEM((2 * SLOT, tile), bf16),
                pltpu.VMEM((heads * rows, 2 * SLOT), f32),
            ],
        ),
        out_shape=[
            jax.ShapeDtypeStruct((SLIM, 128), f32),
            jax.ShapeDtypeStruct((heads * rows, SLOT), f32),
        ],
        compiler_params=params(),
        name="pixels_back",
    )(place, scales, node_row, read_rows, target, eps, weight, decoded)


def backward_kernel(
    d_ref, two_ref, one_ref, norm_ref, up_ref, act_ref, mixed_ref, w_ref, mod_ref, wdec_ref,
    done_ref, dmix_ref, grad_ref, gdec_ref, gmod_ref,
):
    heads, width = w_ref.shape[0], w_ref.shape[1]
    step = pl.program_id(0)

    @pl.when(step == 0)
    def _():
        grad_ref[...] = jnp.zeros_like(grad_ref)
        gdec_ref[...] = jnp.zeros_like(gdec_ref)
        gmod_ref[...] = jnp.zeros_like(gmod_ref)

    d_dec = sum(d_ref[h] for h in range(heads)).astype(bf16)
    normed_two, inv_two = standardize(two_ref[...])
    final = normed_two.astype(bf16)
    gdec_ref[...] += contract(d_dec[:, :SLIM], final, 0, 0)
    d_two = norm_back(normed_two, inv_two, contract(d_dec[:, :SLIM], wdec_ref[...], 1, 0))
    d_low = d_two.astype(bf16)
    norm_two = norm_ref[...]
    d_mid = jnp.zeros_like(d_two)
    for h in range(heads):
        act = act_ref[h]
        up = up_ref[h]
        d_act = contract(d_low, w_ref[h, :, width : 2 * width], 1, 0)
        gating = jax.nn.sigmoid(up)
        d_up = (d_act * gating * (1 + up * (1 - gating))).astype(bf16)
        grad_ref[h, :, :width] += contract(norm_two, d_up, 0, 0)
        grad_ref[h, :, width : 2 * width] += contract(d_low, act, 0, 0)
        d_mid += contract(d_up, w_ref[h, :, :width], 1, 1)
    normed_one, inv_one = standardize(one_ref[...])
    gmod_ref[0:1] += jnp.sum(d_mid * normed_one, 0, keepdims=True)
    gmod_ref[1:2] += jnp.sum(d_mid, 0, keepdims=True)
    d_one = d_two + norm_back(normed_one, inv_one, d_mid * (1 + mod_ref[2:3]))
    done_ref[...] = d_one
    one_low = d_one.astype(bf16)
    for h in range(heads):
        dmix_ref[h] = contract(one_low, w_ref[h, :, 2 * width :], 1, 0).astype(bf16)
        grad_ref[h, :, 2 * width :] += contract(one_low, mixed_ref[h], 0, 0)


def backward(d_dec, h_two, h_one, norm_two, up, act, mixed, w_big, modulation, w_dec, tile):
    heads, rows = mixed.shape[:2]
    width = h_one.shape[1]
    row = lambda w: pl.BlockSpec((tile, w), lambda i: (i, 0))
    stack = lambda w: pl.BlockSpec((heads, tile, w), lambda i: (0, i, 0))
    return pl.pallas_call(
        backward_kernel,
        grid=(rows // tile,),
        in_specs=[
            stack(SLOT),
            row(width),
            row(width),
            row(width),
            stack(width),
            stack(width),
            stack(HD),
            whole(w_big.shape),
            whole(modulation.shape),
            whole(w_dec.shape),
        ],
        out_specs=[row(width), stack(HD), whole(w_big.shape), whole((SLIM, width)), whole((8, width))],
        out_shape=[
            jax.ShapeDtypeStruct((rows, width), f32),
            jax.ShapeDtypeStruct((heads, rows, HD), bf16),
            jax.ShapeDtypeStruct(w_big.shape, f32),
            jax.ShapeDtypeStruct((SLIM, width), f32),
            jax.ShapeDtypeStruct((8, width), f32),
        ],
        compiler_params=params(56),
        name="backward",
    )(d_dec, h_two, h_one, norm_two, up, act, mixed, w_big, modulation, w_dec)


def unproject_kernel(dq_ref, self_ref, down_ref, up_ref, norm_ref, w_ref, dn_ref, grad_ref):
    step = pl.program_id(0)

    @pl.when(step == 0)
    def _():
        grad_ref[...] = jnp.zeros_like(grad_ref)

    kv = self_ref[...] + down_ref[...].astype(f32) + up_ref[...].astype(f32)
    both = jnp.concatenate([dq_ref[...], kv.astype(bf16).T], 1)
    dn_ref[...] = contract(both, w_ref[...], 1, 1).astype(bf16)
    grad_ref[...] += contract(norm_ref[...], both, 0, 0)


def unproject(dq, kv_self, from_below, from_above, norm_all, w_attn, tile):
    nodes, width = norm_all.shape
    row = lambda w: pl.BlockSpec((tile, w), lambda i: (i, 0))
    col = pl.BlockSpec((2 * HD, tile), lambda i: (0, i))
    return pl.pallas_call(
        unproject_kernel,
        grid=(nodes // tile,),
        in_specs=[row(HD), col, col, col, row(width), pl.BlockSpec((width, 3 * HD), lambda i: (0, 0))],
        out_specs=[row(width), whole((width, 3 * HD))],
        out_shape=[
            jax.ShapeDtypeStruct((nodes, width), bf16),
            jax.ShapeDtypeStruct((width, 3 * HD), f32),
        ],
        compiler_params=params(),
        name="unproject",
    )(dq, kv_self, from_below, from_above, norm_all, w_attn)


def leave_kernel(dn_ref, zero_ref, done_ref, in_ref, mod_ref, genc_ref, gmod_ref):
    heads = dn_ref.shape[0]
    d_norm = sum(dn_ref[h].astype(f32) for h in range(heads))
    normed, inv = standardize(zero_ref[...])
    gmod_ref[0:1] = jnp.sum(d_norm * normed, 0, keepdims=True)
    gmod_ref[1:2] = jnp.sum(d_norm, 0, keepdims=True)
    gmod_ref[2:] = jnp.zeros_like(gmod_ref[2:])
    d_zero = done_ref[...] + norm_back(normed, inv, d_norm * (1 + mod_ref[0:1]))
    genc_ref[...] = contract(in_ref[...].T, d_zero, 1, 0, highest)


def leave(d_norm, h_zero, d_one, node_in, modulation):
    width = h_zero.shape[1]
    return pl.pallas_call(
        leave_kernel,
        out_shape=[
            jax.ShapeDtypeStruct((2 * SLOT, width), f32),
            jax.ShapeDtypeStruct((8, width), f32),
        ],
        compiler_params=params(),
        name="leave",
    )(d_norm, h_zero, d_one, node_in, modulation)


def eliminate(blocks):
    size = blocks[0].shape[0]
    tiles = [[b[8 * i : 8 * i + 8] for i in range(size // 8)] for b in blocks]
    lane = lax.broadcasted_iota(jnp.int32, (8, size), 1)
    sub = lax.broadcasted_iota(jnp.int32, (8, size), 0)
    pivots = [jnp.zeros((1, size), f32) for _ in blocks]
    for j in range(size):
        first, inside = divmod(j, 8)
        for m in range(len(blocks)):
            row = tiles[m][first][inside : inside + 1]
            pivot = row[:, j : j + 1]
            here = lane[:1] == j
            pivots[m] = jnp.where(here, pivot, pivots[m])
            scaled = jnp.where(here, 1.0, row) * (1.0 / pivot)
            for i in range(first, size // 8):
                old = tiles[m][i]
                new = jnp.where(lane == j, 0.0, old) - old[:, j : j + 1] * scaled
                if i == first:
                    new = jnp.where(
                        sub > inside, new, jnp.where((sub == inside) & (lane == j), 1.0, old)
                    )
                tiles[m][i] = new
    return [jnp.concatenate(t, 0) for t in tiles], pivots


def renew_kernel(gram_ref, product_ref, out_ref, both):
    count, size = gram_ref.shape[:2]
    k = pl.program_id(0)

    @pl.when(k == 0)
    def _():
        both[:, :size] = gram_ref[...]
        both[:, size:] = product_ref[...]

    at = pl.ds(pl.multiple_of(k * BLOCK, BLOCK), BLOCK)
    factors, pivots = eliminate([both[m, at, at] for m in range(count)])
    below = lax.broadcasted_iota(jnp.int32, (size, BLOCK), 0) >= (k + 1) * BLOCK
    lower = lax.broadcasted_iota(jnp.int32, (BLOCK, BLOCK), 1) <= lax.broadcasted_iota(
        jnp.int32, (BLOCK, BLOCK), 0
    )
    for m in range(count):
        factor = jnp.where(lower, factors[m], 0.0)
        panel = contract(both[m, :, at], factor, 1, 1, highest) * lax.rsqrt(pivots[m])
        out_ref[m] = panel[size:]

        @pl.when(k < size // BLOCK - 1)
        def _():
            left = jnp.where(below, panel[:size], 0.0)
            both[m] -= contract(jnp.concatenate([left, panel[size:]], 0), left, 1, 1, highest)


def renew(gram, product):
    count, size = gram.shape[:2]
    return pl.pallas_call(
        renew_kernel,
        grid=(size // BLOCK,),
        in_specs=[whole(gram.shape), whole(gram.shape)],
        out_specs=pl.BlockSpec((count, size, BLOCK), lambda k: (0, 0, k)),
        out_shape=jax.ShapeDtypeStruct(gram.shape, f32),
        scratch_shapes=[pltpu.VMEM((count, 2 * size, size), f32)],
        compiler_params=params(),
        name="renew",
    )(gram, product)


def local(
    prev_state,
    target,
    noise_eps,
    noise_level,
    valid_count,
    neighbours,
    nbr_count,
    pix_node,
    pix_read,
    w_enc,
    w_cond,
    w_dec,
    layer_w,
    soap_first,
    soap_second,
    soap_basis,
    soap_stats,
    enc_first,
    enc_second,
    cond_first,
    cond_second,
    dec_first,
    dec_second,
):
    nodes = nbr_count.shape[0]
    groups = lax.axis_size("node")
    heads = lax.axis_size("head")
    rows = nodes // heads
    reach = 3 * nodes
    block_start = lax.axis_index("node") * nodes
    quarter = lax.axis_index("head")
    width = w_enc.shape[1]
    both = ("head", "node")

    low_w = layer_w.astype(bf16)
    w_attn = lax.all_gather(low_w[0], "node", axis=0, tiled=True)
    big_share = jnp.concatenate([low_w[1], low_w[2], low_w[0, :, 3 * HD :]], 1)
    w_big = lax.all_gather(big_share, both, axis=0, tiled=True).reshape(heads, width, -1)

    noise_sigma, noise_feat = noise_terms(noise_level)
    sig_sq = noise_sigma * noise_sigma
    input_scale = lax.rsqrt(sig_sq + 1.0)
    skip_scale = 1.0 / (sig_sq + 1.0)
    output_scale = noise_sigma * lax.rsqrt(sig_sq + 1.0)
    loss_scale = (sig_sq + 1.0) / sig_sq
    modulation = jnp.dot(noise_feat[None, :], w_cond, precision=highest).reshape(4, width)

    prev_t, target_t, eps_t = prev_state.T, target.T, noise_eps.T
    node_row = pix_node.reshape(1, -1)
    read_rows = pix_read.T
    place = jnp.stack([block_start, quarter * rows, valid_count[0], quarter]).astype(jnp.int32)
    node_in, stat = encode(
        place, jnp.stack([noise_sigma, input_scale]), node_row, prev_t, target_t, eps_t, rows, 1024
    )
    stat_sum = lax.psum(jnp.sum(stat, 1), "node")
    count_sum = stat_sum[SLIM - 1]
    var_weight = 1.0 / (stat_sum[:VARS] / count_sum + norm_eps)
    loss_count = count_sum * VARS

    pad_enc = jnp.zeros((2, SLOT, width), bf16)
    pad_enc = pad_enc.at[:, :VARS].set(w_enc.astype(bf16).reshape(2, VARS, width))
    h_zero, norm_one = enter(node_in, pad_enc.reshape(2 * SLOT, width), modulation)
    norm_all = lax.all_gather(norm_one, "head", axis=0, tiled=True)
    query, keyval = project(norm_all, w_attn, 512)
    below = passed_along(keyval, "node", 1)
    above = passed_along(keyval, "node", -1)

    relative = (neighbours - block_start + nodes) % (nodes * groups)
    live = jnp.arange(NBR)[None, :] < nbr_count[:, None]
    slots = jnp.where(live, relative, -1).reshape(nodes // GROUP, 256)
    counts = count_slots(slots, reach, 8)
    e, mix, mixed_low = attend(query, below, keyval, above, counts, 128, 512)
    mixed = lax.all_to_all(mixed_low.reshape(heads, rows, HD), "head", 0, 0)

    w_dec_t = jnp.zeros((SLIM, width), bf16).at[:VARS].set(w_dec.T.astype(bf16))
    h_one, h_two, norm_two, up, act, dec = forward(mixed, h_zero, w_big, modulation, w_dec_t, 256)
    decoded = lax.all_gather(dec, "head", axis=0)
    scales = jnp.stack(
        [noise_sigma, input_scale, skip_scale, output_scale, output_scale * (2.0 / loss_count) / 3.0]
    )
    weight = jnp.broadcast_to((loss_scale * var_weight)[:, None], (VARS, 128))
    loss_part, d_part = pixels_back(
        place, scales, node_row, read_rows, target_t, eps_t, weight, decoded, 512
    )
    d_dec = lax.all_to_all(d_part.reshape(heads, rows, SLOT), "head", 0, 0)
    d_one, d_mixed, grad_big, grad_dec, gmod_two = backward(
        d_dec, h_two, h_one, norm_two, up, act, mixed, w_big, modulation, w_dec_t, 256
    )
    big_share = lax.psum_scatter(
        grad_big.reshape(heads * width, -1), both, scatter_dimension=0, tiled=True
    )
    d_mixed = lax.all_to_all(d_mixed, "head", 0, 0).reshape(nodes, HD)
    dq, kv_low, kv_self, kv_high = attend_back(
        query, d_mixed, mix, e, below, keyval, above, 256, 512
    )
    from_above = passed_along(kv_low, "node", -1)
    from_below = passed_along(kv_high, "node", 1)
    dn_part, grad_qkv = unproject(dq, kv_self, from_below, from_above, norm_all, w_attn, 512)
    qkv_share = lax.psum_scatter(grad_qkv, "node", scatter_dimension=0, tiled=True)
    d_norm = lax.all_to_all(dn_part.reshape(heads, rows, width), "head", 0, 0)
    grad_enc, gmod_one = leave(d_norm, h_zero, d_one, node_in, modulation)

    grad_enc = jnp.concatenate([grad_enc[:VARS], grad_enc[SLOT : SLOT + VARS]], 0)
    d_mod = jnp.concatenate([gmod_one[:2], gmod_two[:2]], 0)
    grad_enc, d_mod, grad_dec = lax.psum((grad_enc, d_mod, grad_dec[:VARS]), both)
    grad_cond = noise_feat[:, None] * d_mod.reshape(1, -1)
    layer_share = jnp.stack(
        [
            jnp.concatenate([qkv_share, big_share[:, 2 * width :]], 1),
            big_share[:, :width],
            big_share[:, width : 2 * width],
        ]
    )
    small_sq = (
        jnp.sum(grad_enc * grad_enc) + jnp.sum(grad_cond * grad_cond) + jnp.sum(grad_dec * grad_dec)
    )
    total_sq, loss_sum = lax.psum((jnp.sum(layer_share * layer_share), jnp.sum(loss_part[:VARS])), both)
    grad_norm = jnp.sqrt(total_sq + small_sq)
    clip_factor = clip_limit / jnp.maximum(grad_norm, clip_limit)
    clipped = clip_factor * layer_share
    grad_full = lax.all_gather(layer_share, "node", axis=1, tiled=True)
    raw_stat = jnp.einsum("idb,idc->ibc", grad_full, grad_full, precision=highest)
    stat_new = clip_factor * (clip_factor * raw_stat)
    basis_old = soap_basis[:, 0]
    rotated = jnp.einsum("idb,ibc->idc", clipped, basis_old, precision=highest)
    first_new = beta_first * soap_first + (1 - beta_first) * rotated
    second_new = beta_second * soap_second + (1 - beta_second) * rotated * rotated
    direction = (
        first_new
        / (1 - beta_first**STEP)
        / (jnp.sqrt(second_new / (1 - beta_second**STEP)) + adam_epsilon)
    )
    step_back = jnp.einsum("idc,ibc->idb", direction, basis_old, precision=highest)
    layer_new = layer_w - rate_layer * (step_back + decay_rate * layer_w)
    stats_new = beta_stats * soap_stats[:, 0] + (1 - beta_stats) * stat_new
    product = jnp.einsum("ibc,icd->ibd", stats_new, basis_old, precision=highest)
    gram_matrix = jnp.einsum("ibc,ibd->icd", product, product, precision=highest)
    basis_new = renew(gram_matrix, product)
    enc_new = adam_small(w_enc, clip_factor * grad_enc, enc_first, enc_second)
    cond_new = adam_small(w_cond, clip_factor * grad_cond, cond_first, cond_second)
    dec_new = adam_small(w_dec.T, clip_factor * grad_dec, dec_first.T, dec_second.T)
    return (
        jnp.reshape(loss_sum, (1,)),
        jnp.reshape(loss_count, (1,)),
        jnp.reshape(grad_norm, (1,)),
        layer_new,
        first_new,
        second_new,
        basis_new[:, None],
        stats_new[:, None],
        *enc_new,
        *cond_new,
        *(x.T for x in dec_new),
    )


def solution(mesh):
    pixel = P("node", None)
    layer = P(None, "node", "head")
    basis = P(None, "head", None, None)
    placed = (
        *(pixel,) * 3,
        P(),
        P("node"),
        P("node", None),
        P("node"),
        P("node"),
        P("node", None),
        *(P(),) * 3,
        *(layer,) * 3,
        *(basis,) * 2,
        *(P(),) * 6,
    )
    return jax.shard_map(
        local,
        mesh=mesh,
        in_specs=placed,
        out_specs=(*(P(),) * 3, *(layer,) * 3, *(basis,) * 2, *(P(),) * 9),
        check_vma=False,
    )
```

time: 2280 us -> 763 us (0.33)
  other arithmetic: 994 us -> 18.1 us
  local copies, waits for them, and re-layouts: 488 us -> 26 us
  waiting for transfers between devices: 540 us -> 279 us
  Pallas kernels: 0 us -> 229 us
  matrix products: 160 us -> 27.1 us
  blocking collectives: 54.6 us -> 135 us
    scatter-add x3 -> x0, other arithmetic: 452 us -> none  [the longest x1 197 us: local(): jax.ops.segment_sum(jnp.repeat(d_field / 3.0, 3, axis=0), read_local.resh...]
    another operation x28 -> x4, other arithmetic: 422 us -> 3.36 us  [the longest x2 3.2 us: local(): jnp.stack([jnp.concatenate([qkv_share, big_share[:, 2 * width:]], 1), big...]
    psum x6 -> x1, waiting for transfers between devices: 453 us -> 128 us  [local(): lax.psum((grad_enc, d_mod, grad_dec[:VARS]), both)]
    gather x7 -> x0, local copies, waits for them, and re-layouts: 268 us -> none  [the longest x1 123 us: local(): near_rows = source[row_index].reshape(node_rows, NBR, heads_here, 2, HD)]
    pallas_call x0 -> x12, Pallas kernels: none -> 229 us  [the longest x1 75.4 us: renew(): pl.pallas_call(renew_kernel, grid=(size // BLOCK,), in_specs=[whole(gram....]
    dot_general x23 -> x2, matrix products: 108 us -> 10.2 us  [the longest x1 8.97 us: local(): jnp.einsum('idb,idc->ibc', grad_full, grad_full, precision=highest)]
    reshape x3 -> x1, local copies, waits for them, and re-layouts: 55.1 us -> 1.61 us  [local(): slots = jnp.where(live, relative, -1).reshape(nodes // GROUP, 256)]
    all_to_all x0 -> x2, waiting for transfers between devices: none -> 37.4 us  [the longest x1 32.2 us: local(): d_norm = lax.all_to_all(dn_part.reshape(heads, rows, width), 'head', 0, 0)]
  transfers between devices with their start and end apart: 12 -> 12, of which waited for: 10 -> 8; matrix products, arithmetic and copies ran while one was open for 9% -> 4% of each run, Pallas kernels for 0% -> 13%
where the time goes in v1:
time: 763 us; the launch traced here: 753 us
  waiting for transfers between devices  279 us (37%)
  Pallas kernels  229 us (30%)
  blocking collectives  135 us (18%)
  matrix products  27.1 us (4%)
  local copies, waits for them, and re-layouts  26 us (3%)
  between operations  22.5 us (3%)
  other arithmetic  18.1 us (2%)
  starting transfers between devices  16.3 us (2%)
    psum x1, waiting for transfers between devices, local(): lax.psum((grad_enc, d_mod, grad_dec[:VARS]), both)  128 us
    pallas_call x1, Pallas kernels, renew(): pl.pallas_call(renew_kernel, grid=(size // BLOCK,), in_specs=[whole(gram....  75.4 us
    ppermute x4, waiting for transfers between devices, passed_along(): lax.ppermute(x, axis, [(i, (i + by) % length) for i in range(length)])  42.1 us
    psum x1, blocking collectives, local(): lax.psum((jnp.sum(layer_share * layer_share), jnp.sum(loss_part[:VARS])),...  41.3 us
    psum x1, blocking collectives, local(): stat_sum = lax.psum(jnp.sum(stat, 1), 'node')  39.7 us
    pallas_call x1, Pallas kernels, attend_back(): pl.pallas_call(functools.partial(attend_back_kernel, chunk=chunk), grid=(...  36.6 us
    pallas_call x1, Pallas kernels, attend(): pl.pallas_call(functools.partial(attend_kernel, chunk=chunk), grid=(nodes...  35.7 us
    all_to_all x1, waiting for transfers between devices, local(): d_norm = lax.all_to_all(dn_part.reshape(heads, rows, width), 'head', 0, 0)  32.2 us
  transfers between devices with their start and end apart: 12, of which 8 were waited for; matrix products, arithmetic and copies ran while one was open for 4% of the time, Pallas kernels for 13%

profile of v1, /device:TPU:0, one launch (start us, length us, event | category | flops | bytes accessed | tf_op | source)
XLA Modules:
  0.0 753.4 jit_solution(17527176706526323840)
XLA Ops:
  14.6 10.8 %encode.1 = (f32[512,256]{1,0:T(8,128)S(1)}, f32[96,128]{1,0:T(8,128)S(1)}) custom-call(s32[4]{0:T(128)S(1)} %pad_add_fusion.place_ref, f32[2]{0:T(128)S(1)} %pad_maximum_fusion.3.scale_ref, s32[1,12288]{1,0:T(1,128)S(1)} %bitcast.126, f32[84,12288]{1,0:T(8,128)S(1)} %bitcast.117, f32[84,12288]{1,0:T(8,128)} %bitcast.131, f32[84,12288]{1,0:T(8,128)} %bitcast.133), custom_call_target="tpu_custom_call" | custom-call | tf_op jit(solution)/shard_map/encode/pallas_call | solution.py:149
  29.9 17.6 %all-gather = bf16[1,512,512]{2,1,0:T(8,128)(2,1)} all-gather(bf16[1,64,512]{2,1,0:T(8,128)(2,1)S(1)} %get-tuple-element.159), channel_id=2, replica_groups=mesh['head'=4,'node'=8] {'node'}, dimensions={1}, use_global_device_ids=true | all-gather | bytes 589824 | tf_op jit(solution)/shard_map/all_gather | solution.py:702
  47.5 18.8 %all-gather.6.cloned.1.call-done.norm_ref = bf16[2048,512]{1,0:T(8,128)(2,1)} async-done(((bf16[512,512]{1,0:T(8,128)(2,1)}), bf16[2048,512]{1,0:T(8,128)(2,1)}) %all-gather.6.cloned.1.call-update) | async-done | bytes 2097168 | tf_op jit(solution)/shard_map/all_gather | solution.py:729
  76.2 39.7 %psum.42 = f32[96]{0:T(128)S(1)} all-reduce(f32[96]{0:T(128)S(1)} %reduce_sum.54), channel_id=1, replica_groups=mesh['head'=4,'node'=8] {'node'}, use_global_device_ids=true, to_apply=%region_1.0 | all-reduce | flops 96 | bytes 768 | tf_op jit(solution)/shard_map/psum | solution.py:721
  119.5 15.0 %count_slots.1.count_ref = bf16[2048,6144]{1,0:T(8,128)(2,1)} custom-call(s32[128,256]{1,0:T(8,128)S(1)} %reshape.153.slot_ref), custom_call_target="tpu_custom_call" | custom-call | tf_op jit(solution)/shard_map/count_slots/pallas_call | solution.py:234
  134.5 35.7 %attend.1 = (bf16[2048,6144]{1,0:T(8,128)(2,1)}, f32[2048,256]{1,0:T(8,128)}, bf16[2048,128]{1,0:T(8,128)(2,1)}) custom-call(bf16[2048,128]{1,0:T(8,128)(2,1)} %copy-done.8, bf16[2048,256]{1,0:T(8,128)(2,1)} %collective-permute-done.below_ref, bf16[2048,256]{1,0:T(8,128)(2,1)} %get-tuple-element.75.here_ref, ...), custom_call_target="tpu_custom_call" | custom-call | tf_op jit(solution)/shard_map/attend/pallas_call | solution.py:279
  175.9 5.2 all-to-all-done.mixed_ref
  182.4 9.4 %forward.1 = (f32[512,512]{1,0:T(8,128)S(1)}, f32[512,512]{1,0:T(8,128)S(1)}, bf16[512,512]{1,0:T(8,128)(2,1)S(1)}, f32[4,512,512]{2,1,0:T(8,128)}, bf16[4,512,5...) custom-call(bf16[4,512,128]{2,1,0:T(8,128)(2,1)} %all-to-all-done.mixed_ref, f32[512,512]{1,0:T(8,128)S(1)} %copy-done.6, ...), custom_call_target="tpu_custom_call" | custom-call | tf_op jit(solution)/shard_map/forward/pallas_call | solution.py:383
  193.7 11.8 %all-gather.1 = bf16[768,512]{1,0:T(8,128)(2,1)S(1)} all-gather(bf16[192,512]{1,0:T(8,128)(2,1)S(1)} %get-tuple-element.78), channel_id=3, replica_groups=mesh['head'=4,'node'=8] {'head'}, dimensions={0}, use_global_device_ids=true | all-gather | bytes 983040 | tf_op jit(solution)/shard_map/all_gather | solution.py:743
  205.6 16.7 %pixels_back.1 = (f32[96,128]{1,0:T(8,128)S(1)}, f32[2048,128]{1,0:T(8,128)S(1)}) custom-call(s32[4]{0:T(128)S(1)} %pad_add_fusion.place_ref, f32[5]{0:T(128)S(1)} %stack.54.scale_ref, s32[1,12288]{1,0:T(1,128)S(1)} %bitcast.127, s32[3,12288]{1,0:T(4,128)S(1)} %bitcast.128, f32[84,12288]{1,0:T(8,128)} %bitcast.132, f32[84,12288]{1,0:T(8,128)} %bitcast.134, ...), custom_call_target="tpu_custom_call" | custom-call | tf_op jit(solution)/shard_map/pixels_back/pallas_call | solution.py:442
  222.3 13.8 %all_to_all.20.d_ref = f32[4,512,128]{2,1,0:T(8,128)} all-to-all(f32[4,512,128]{2,1,0:T(8,128)S(1)} %bitcast.121), channel_id=1, replica_groups=mesh['head'=4,'node'=8] {'head'}, dimensions={0} | all-to-all | bytes 2097152 | tf_op jit(solution)/shard_map/all_to_all | solution.py:751
  236.1 17.0 %backward.1 = (f32[512,512]{1,0:T(8,128)}, bf16[4,512,128]{2,1,0:T(8,128)(2,1)}, f32[4,512,1152]{2,1,0:T(8,128)}, f32[96,512]{1,0:T(8,128)}, f32[8,512]{1,0:T(8,128)}) custom-call(f32[4,512,128]{2,1,0:T(8,128)} %all_to_all.20.d_ref, f32[512,512]{1,0:T(8,128)} %copy-done.13, f32[512,512]{1,0:T(8,128)} %copy-done.12, bf16[512,512]{1,0:T(8,128)(2,1)} %copy-done.18, ...), custom_call_target="tpu_custom_call" | custom-call | tf_op jit(solution)/shard_map/backward/pallas_call | solution.py:518
  253.1 11.3 %all_to_all.21 = bf16[4,512,128]{2,1,0:T(8,128)(2,1)} all-to-all(bf16[4,512,128]{2,1,0:T(8,128)(2,1)} %get-tuple-element.86), channel_id=1, replica_groups=mesh['head'=4,'node'=8] {'head'}, dimensions={0} | all-to-all | bytes 1048576 | tf_op jit(solution)/shard_map/all_to_all | solution.py:758
  264.5 36.6 %attend_back.1 = (bf16[2048,128]{1,0:T(8,128)(2,1)}, bf16[256,2048]{1,0:T(8,128)(2,1)}, f32[256,2048]{1,0:T(8,128)}, bf16[256,2048]{1,0:T(8,128)(2,1)}) custom-call(bf16[2048,128]{1,0:T(8,128)(2,1)} %copy-done.8, bf16[2048,128]{1,0:T(8,128)(2,1)} %bitcast.138, f32[2048,256]{1,0:T(8,128)} %get-tuple-element.87.mix_ref, ...), custom_call_target="tpu_custom_call" | custom-call | tf_op jit(solution)/shard_map/attend_back/pallas_call | solution.py:338
  304.6 37.0 %collective-permute-done.2.down_ref = bf16[256,2048]{1,0:T(8,128)(2,1)S(1)} collective-permute-done((bf16[256,2048]{1,0:T(8,128)(2,1)}, bf16[256,2048]{1,0:T(8,128)(2,1)S(1)}, u32[]{:S(2)}, u32[]{:S(2)}) %collective-permute-start.2) | collective-permute-done | bytes 1048608 | tf_op jit(solution)/shard_map/ppermute | solution.py:41
  361.1 32.2 %all-to-all-done.3.dn_ref = bf16[4,512,512]{2,1,0:T(8,128)(2,1)} async-done(((bf16[4,512,512]{2,1,0:T(8,128)(2,1)}), bf16[4,512,512]{2,1,0:T(8,128)(2,1)}, u32[]{:S(2)}, u32[]{:S(2)}) %all-to-all-start.3) | async-done | bytes 2097184 | tf_op jit(solution)/shard_map/all_to_all | solution.py:766
  401.2 22.2 %reduce-scatter.5.cloned.1.call-done = f32[64,1152]{1,0:T(8,128)} async-done(((f32[2048,1152]{1,0:T(8,128)}), f32[64,1152]{1,0:T(8,128)}) %reduce-scatter.5.cloned.1.call-update) | async-done | bytes 294928 | tf_op jit(solution)/shard_map/reduce_scatter | solution.py:755
  425.7 30.9 %reduce-scatter.3.cloned.1.call-done = f32[64,384]{1,0:T(8,128)} async-done(((f32[512,384]{1,0:T(8,128)}), f32[64,384]{1,0:T(8,128)}) %reduce-scatter.3.cloned.1.call-update) | async-done | bytes 98320 | tf_op jit(solution)/shard_map/reduce_scatter | solution.py:765
  461.2 127.5 %all-reduce.6.cloned.1.call-done = (f32[168,512]{1,0:T(8,128)}, f32[84,512]{1,0:T(8,128)}) async-done(((f32[168,512]{1,0:T(8,128)}, f32[84,512]{1,0:T(8,128)}), (f32[168,512]{1,0:T(8,128)}, f32[84,512]{1,0:T(8,128)})) %all-reduce.6.cloned.1.call-update) | async-done | bytes 516112 | tf_op jit(solution)/shard_map/psum | solution.py:771
  592.0 41.3 %all-reduce.2 = (f32[1]{0:T(128)}, f32[]{:T(128)}, f32[2048]{0:T(1024)S(1)}) all-reduce(f32[1]{0:T(128)} %bitcast.27, f32[]{:T(128)} %get-tuple-element.149, f32[2048]{0:T(1024)S(1)} %bitcast.141), channel_id=1, replica_groups=mesh['head'=4,'node'=8] {'head','node'}, use_global_device_ids=true, to_apply=%region_3.4 | all-reduce | flops 2050 | bytes 16400 | tf_op jit(solution)/shard_map/psum | solution.py:783
  648.5 9.0 %bitcast_add_fusion = f32[3,512,512]{2,1,0:T(8,128)S(1)} fusion(f32[3,1,512,512]{3,2,1,0:T(8,128)} %param.43, f32[3,512,512]{2,1,0:T(8,128)} %all-gather.10.cloned.1.call-done, f32[]{:T(128)S(6)} %div.96), kind=kOutput, calls=%fused_computation | convolution fusion | flops 4835770368 | bytes 9437188 | tf_op jit(solution)/shard_map/idb,idc->ibc/dot_general | solution.py:788
  657.5 5.5 fusion.product_ref
  663.0 5.5 fusion.52.gram_ref
  668.5 75.4 %renew.1 = f32[3,512,512]{2,1,0:T(8,128)} custom-call(f32[3,512,512]{2,1,0:T(8,128)S(1)} %fusion.52.gram_ref, f32[3,512,512]{2,1,0:T(8,128)} %copy-done.25), custom_call_target="tpu_custom_call" | custom-call | tf_op jit(solution)/shard_map/renew/pallas_call | solution.py:654
  (150 shorter events, 85.4 us)
Async XLA Ops:
  7.2 634.1 %copy-start = (f32[3,1,512,512]{3,2,1,0:T(8,128)S(1)}, f32[3,1,512,512]{3,2,1,0:T(8,128)}, u32[]{:S(2)}) copy-start(f32[3,1,512,512]{3,2,1,0:T(8,128)} %param.42) | copy-start | bytes 9437188
  7.2 59.0 %all-gather.6.cloned.1.call-start = ((), (), s32[]{:S(2)}) async-start(), calls=%async_computation.6 | async-start | bytes 2621440 | tf_op jit(solution)/shard_map/all_gather | solution.py:729
  11.4 169.7 %copy-start.20 = (f32[1,4,512]{2,1,0:T(4,128)}, f32[1,4,512]{2,1,0:T(4,128)S(1)}, u32[]{:S(2)}) copy-start(f32[1,4,512]{2,1,0:T(4,128)S(1)} %copy.60) | copy-start | bytes 24580
  25.4 91.1 %copy-start.38 = (s32[2048,16]{0,1:T(8,128)S(1)}, s32[2048,16]{0,1:T(8,128)}, u32[]{:S(2)}) copy-start(s32[2048,16]{0,1:T(8,128)} %param.32) | copy-start | bytes 393220
  25.4 91.1 %copy-start.39 = (s32[2048]{0:T(1024)S(1)}, s32[2048]{0:T(1024)}, u32[]{:S(2)}) copy-start(s32[2048]{0:T(1024)} %param.33) | copy-start | bytes 24580
  28.1 153.0 %all-gather.8.cloned.1.call-start = ((), (), s32[]{:S(2)}) async-start(), calls=%async_computation.7 | async-start | bytes 4866048 | tf_op jit(solution)/shard_map/all_gather | solution.py:704
  72.5 62.0 %collective-permute-start = (bf16[2048,256]{1,0:T(8,128)(2,1)}, bf16[2048,256]{1,0:T(8,128)(2,1)}, u32[]{:S(2)}, u32[]{:S(2)}) collective-permute-start(bf16[2048,256]{1,0:T(8,128)(2,1)} %get-tuple-element.75.here_ref), channel_id=1, source_target_pairs={{0,1},{1,2},{2,3},{3,4},{4,5},{5,6},{6,7},{7,0},{8,9},{9,10},{10,1... | collective-permute-start | bytes 3145736 | tf_op jit(solution)/shard_map/ppermute | solution.py:41
  72.5 62.0 %collective-permute-start.1 = (bf16[2048,256]{1,0:T(8,128)(2,1)}, bf16[2048,256]{1,0:T(8,128)(2,1)}, u32[]{:S(2)}, u32[]{:S(2)}) collective-permute-start(bf16[2048,256]{1,0:T(8,128)(2,1)} %get-tuple-element.75.here_ref), channel_id=1, source_target_pairs={{0,7},{1,0},{2,1},{3,2},{4,3},{5,4},{6,5},{7,6},{8,15},{9,8},{10,9... | collective-permute-start | bytes 3145736 | tf_op jit(solution)/shard_map/ppermute | solution.py:41
  134.5 39.9 %copy-start.32 = (f32[512,84]{0,1:T(8,128)S(1)}, f32[512,84]{0,1:T(8,128)}, u32[]{:S(2)}) copy-start(f32[512,84]{0,1:T(8,128)} %param.38) | copy-start | bytes 516100
  170.2 10.9 %all-to-all-start = ((bf16[4,512,128]{2,1,0:T(8,128)(2,1)}), bf16[4,512,128]{2,1,0:T(8,128)(2,1)}, u32[]{:S(2)}, u32[]{:S(2)}) async-start(bf16[4,512,128]{2,1,0:T(8,128)(2,1)} %bitcast.140), calls=%async_computation | async-start | bytes 1048576 | tf_op jit(solution)/shard_map/all_to_all | solution.py:739
  174.3 249.0 %reduce-scatter.5.cloned.1.call-start = ((), (), s32[]{:S(2)}) async-start(), calls=%async_computation.9 | async-start | bytes 9732096 | tf_op jit(solution)/shard_map/reduce_scatter | solution.py:755
  174.4 17.3 %copy-start.15 = (bf16[96,512]{1,0:T(8,128)(2,1)}, bf16[96,512]{1,0:T(8,128)(2,1)S(1)}, u32[]{:S(2)}) copy-start(bf16[96,512]{1,0:T(8,128)(2,1)S(1)} %scatter.9.wdec_ref) | copy-start | bytes 294916
  182.3 23.2 %copy-start.23 = (s32[12288]{0:T(1024)S(1)}, s32[12288]{0:T(1024)}, u32[]{:S(2)}) copy-start(s32[12288]{0:T(1024)} %param.34) | copy-start | bytes 147460
  182.4 23.2 %copy-start.24 = (s32[12288,3]{0,1:T(4,128)S(1)}, s32[12288,3]{0,1:T(4,128)}, u32[]{:S(2)}) copy-start(s32[12288,3]{0,1:T(4,128)} %param.35) | copy-start | bytes 442372
  193.7 28.5 %copy-start.18 = (bf16[512,512]{1,0:T(8,128)(2,1)}, bf16[512,512]{1,0:T(8,128)(2,1)S(1)}, u32[]{:S(2)}) copy-start(bf16[512,512]{1,0:T(8,128)(2,1)S(1)} %get-tuple-element.83.norm_ref) | copy-start | bytes 1572868
  264.5 82.3 %copy-start.3 = (bf16[1,512,512]{2,1,0:T(8,128)(2,1)S(1)}, bf16[1,512,512]{2,1,0:T(8,128)(2,1)}, u32[]{:S(2)}) copy-start(bf16[1,512,512]{2,1,0:T(8,128)(2,1)} %all-gather) | copy-start | bytes 1572868
  301.1 40.6 %collective-permute-start.2 = (bf16[256,2048]{1,0:T(8,128)(2,1)}, bf16[256,2048]{1,0:T(8,128)(2,1)S(1)}, u32[]{:S(2)}, u32[]{:S(2)}) collective-permute-start(bf16[256,2048]{1,0:T(8,128)(2,1)} %get-tuple-element.91), channel_id=1, source_target_pairs={{0,1},{1,2},{2,3},{3,4},{4,5},{5,6},{6,7},{7,0},{8,9},{9,10},{10,1... | collective-permute-start | bytes 3145736 | tf_op jit(solution)/shard_map/ppermute | solution.py:41
  301.1 45.7 %collective-permute-start.3 = (bf16[256,2048]{1,0:T(8,128)(2,1)}, bf16[256,2048]{1,0:T(8,128)(2,1)S(1)}, u32[]{:S(2)}, u32[]{:S(2)}) collective-permute-start(bf16[256,2048]{1,0:T(8,128)(2,1)} %get-tuple-element.92), channel_id=1, source_target_pairs={{0,7},{1,0},{2,1},{3,2},{4,3},{5,4},{6,5},{7,6},{8,15},{9,8},{10,9... | collective-permute-start | bytes 3145736 | tf_op jit(solution)/shard_map/ppermute | solution.py:41
  355.0 38.3 %copy-start.21 = (f32[1,4,512]{2,1,0:T(4,128)S(1)}, f32[1,4,512]{2,1,0:T(4,128)}, u32[]{:S(2)}) copy-start(f32[1,4,512]{2,1,0:T(4,128)} %copy-done.20) | copy-start | bytes 24580
  355.0 38.3 %all-to-all-start.3 = ((bf16[4,512,512]{2,1,0:T(8,128)(2,1)}), bf16[4,512,512]{2,1,0:T(8,128)(2,1)}, u32[]{:S(2)}, u32[]{:S(2)}) async-start(bf16[4,512,512]{2,1,0:T(8,128)(2,1)} %bitcast.119), calls=%async_computation.5 | async-start | bytes 4194304 | tf_op jit(solution)/shard_map/all_to_all | solution.py:766
  359.6 97.0 %reduce-scatter.3.cloned.1.call-start = ((), (), s32[]{:S(2)}) async-start(), calls=%async_computation.8 | async-start | bytes 884736 | tf_op jit(solution)/shard_map/reduce_scatter | solution.py:765
  360.2 228.5 %all-reduce.6.cloned.1.call-start = ((), (), s32[]{:S(2)}) async-start(), calls=%async_computation.11 | async-start | bytes 1048576 | tf_op jit(solution)/shard_map/psum | solution.py:771
  401.1 247.4 %all-gather.10.cloned.1.call-start = ((), (), s32[]{:S(2)}) async-start(), calls=%async_computation.10 | async-start | bytes 3538944 | tf_op jit(solution)/shard_map/all_gather | solution.py:787
  657.5 5.5 copy-start.26
  (28 other events, 65.9 us)
Sparse Core Ops, SparseCore 0:
  28.2 37.9 all-gather.5
  69.8 64.9 all-gather.7
  253.3 170.0 reduce-scatter.4
  426.2 30.4 reduce-scatter.2
  462.3 126.3 all-reduce.5
  590.9 38.3 all-gather.9

commit v2 on v1

--- a/solution.py
+++ b/solution.py
@@ -574,28 +574,173 @@
     )(dq, kv_self, from_below, from_above, norm_all, w_attn)
 
 
-def leave_kernel(dn_ref, zero_ref, done_ref, in_ref, mod_ref, genc_ref, gmod_ref):
+def settle_kernel(
+    feat_ref, dn_ref, zero_ref, done_ref, in_ref, mod_ref, gdec_ref, gmod_ref, qkv_ref, big_ref, loss_ref,
+    small_ref, share_ref, full_ref, sums_ref,
+    parts, spread, inbox, pay, heard, q_low, q_box, sems,
+):
     heads = dn_ref.shape[0]
+    nodes = q_low.shape[0]
+    world = inbox.shape[0]
+    head, node = lax.axis_index("head"), lax.axis_index("node")
+    me = head * nodes + node
+    share_rows = share_ref.shape[0]
+    a_send, a_recv, q_send, q_recv, b_send, b_recv, f_send, f_recv = (sems.at[i] for i in range(8))
+
+    def where(other):
+        return {"head": other // nodes, "node": other % nodes}
+
+    barrier = pltpu.get_barrier_semaphore()
+
+    def greet(off, carry):
+        pl.semaphore_signal(barrier, inc=1, device_id=where((me + off) % world))
+        return carry
+
+    lax.fori_loop(1, world, greet, 0)
+    for t in range(nodes):
+        q_low[t] = qkv_ref[t * share_rows : (t + 1) * share_rows].astype(bf16)
+    pl.semaphore_wait(barrier, world - 1)
+
+    def q_copy(off):
+        other = (node + off) % nodes
+        return pltpu.make_async_remote_copy(
+            src_ref=q_low.at[other],
+            dst_ref=q_box.at[node],
+            send_sem=q_send.at[other],
+            recv_sem=q_recv.at[node],
+            device_id={"node": other},
+        )
+
+    def q_arrived(off):
+        other = (node + off) % nodes
+        return pltpu.make_async_remote_copy(
+            src_ref=q_low.at[other],
+            dst_ref=q_box.at[other],
+            send_sem=q_send.at[other],
+            recv_sem=q_recv.at[other],
+            device_id={"node": other},
+        )
+
+    def each(count, act):
+        def body(off, carry):
+            act(off)
+            return carry
+
+        lax.fori_loop(1, count, body, 0)
+
+    each(nodes, lambda off: q_copy(off).start())
+
     d_norm = sum(dn_ref[h].astype(f32) for h in range(heads))
     normed, inv = standardize(zero_ref[...])
-    gmod_ref[0:1] = jnp.sum(d_norm * normed, 0, keepdims=True)
-    gmod_ref[1:2] = jnp.sum(d_norm, 0, keepdims=True)
-    gmod_ref[2:] = jnp.zeros_like(gmod_ref[2:])
     d_zero = done_ref[...] + norm_back(normed, inv, d_norm * (1 + mod_ref[0:1]))
-    genc_ref[...] = contract(in_ref[...].T, d_zero, 1, 0, highest)
-
-
-def leave(d_norm, h_zero, d_one, node_in, modulation):
-    width = h_zero.shape[1]
-    return pl.pallas_call(
-        leave_kernel,
+    g_enc = contract(in_ref[...].T, d_zero, 1, 0, highest)
+    parts[...] = jnp.zeros_like(parts)
+    parts[:VARS] = g_enc[:VARS]
+    parts[VARS : 2 * VARS] = g_enc[SLOT : SLOT + VARS]
+    parts[2 * VARS : 3 * VARS] = gdec_ref[:VARS]
+    at = 3 * VARS
+    parts[at : at + 1] = jnp.sum(d_norm * normed, 0, keepdims=True)
+    parts[at + 1 : at + 2] = jnp.sum(d_norm, 0, keepdims=True)
+    parts[at + 2 : at + 4] = gmod_ref[0:2]
+    for t in range(world):
+        spread[t] = parts[8 * t : 8 * t + 8]
+
+    def a_copy(off, slot):
+        other = (me + off) % world
+        return pltpu.make_async_remote_copy(
+            src_ref=spread.at[other],
+            dst_ref=inbox.at[slot(other)],
+            send_sem=a_send.at[other],
+            recv_sem=a_recv.at[slot(other)],
+            device_id=where(other),
+        )
+
+    def b_copy(off, slot):
+        other = (me + off) % world
+        return pltpu.make_async_remote_copy(
+            src_ref=pay,
+            dst_ref=heard.at[slot(other)],
+            send_sem=b_send.at[other],
+            recv_sem=b_recv.at[slot(other)],
+            device_id=where(other),
+        )
+
+    mine = lambda other: me
+    theirs = lambda other: other
+    each(world, lambda off: a_copy(off, mine).start())
+
+    each(nodes, lambda off: q_arrived(off).wait_recv())
+    q_box[node] = q_low[node]
+    share = sum(q_box[t].astype(f32) for t in range(nodes))
+    share_ref[...] = share
+    each(nodes, lambda off: q_copy(off).wait_send())
+    q_low[0] = share.astype(bf16)
+
+    def f_copy(off, slot):
+        other = (node + off) % nodes
+        return pltpu.make_async_remote_copy(
+            src_ref=q_low.at[0],
+            dst_ref=full_ref.at[slot(other)],
+            send_sem=f_send.at[other],
+            recv_sem=f_recv.at[slot(other)],
+            device_id={"node": other},
+        )
+
+    each(nodes, lambda off: f_copy(off, lambda other: node).start())
+    full_ref[node] = share.astype(bf16)
+
+    each(world, lambda off: a_copy(off, theirs).wait_recv())
+    inbox[me] = spread[me]
+    own = sum(inbox[t] for t in range(world))
+    row = lax.broadcasted_iota(jnp.int32, own.shape, 0) + 8 * me
+    weighted = own * own * jnp.where(row >= 3 * VARS, feat_ref[0], 1.0)
+    total = jnp.sum(weighted) + jnp.sum(share * share) + jnp.sum(big_ref[...] * big_ref[...])
+    loss = jnp.sum(loss_ref[:VARS])
+    width = own.shape[1]
+    pay[:, :width] = own
+    line = lax.broadcasted_iota(jnp.int32, (8, 128), 0)
+    pay[:, width:] = jnp.where(line == 0, total, jnp.where(line == 1, loss, 0.0))
+    each(world, lambda off: b_copy(off, mine).start())
+    heard[me] = pay[...]
+    each(world, lambda off: b_copy(off, theirs).wait_recv())
+    for t in range(world):
+        small_ref[8 * t : 8 * t + 8] = heard[t, :, :width]
+    sums_ref[...] = sum(heard[t, :, width:] for t in range(world))
+    each(nodes, lambda off: f_copy(off, lambda other: other).wait_recv())
+    each(world, lambda off: a_copy(off, mine).wait_send())
+    each(world, lambda off: b_copy(off, mine).wait_send())
+    each(nodes, lambda off: f_copy(off, lambda other: node).wait_send())
+
+
+def settle(feat_sq, d_norm, h_zero, d_one, node_in, modulation, grad_dec, gmod_two, grad_qkv, big_share, loss, nodes):
+    heads, rows, width = d_norm.shape
+    world = heads * nodes
+    share = (grad_qkv.shape[0] // nodes, grad_qkv.shape[1])
+    return pl.pallas_call(
+        settle_kernel,
+        in_specs=[smem()] + [pl.BlockSpec(memory_space=pltpu.VMEM)] * 10,
+        out_specs=[pl.BlockSpec(memory_space=pltpu.VMEM)] * 4,
         out_shape=[
-            jax.ShapeDtypeStruct((2 * SLOT, width), f32),
-            jax.ShapeDtypeStruct((8, width), f32),
-        ],
-        compiler_params=params(),
-        name="leave",
-    )(d_norm, h_zero, d_one, node_in, modulation)
+            jax.ShapeDtypeStruct((8 * world, width), f32),
+            jax.ShapeDtypeStruct(share, f32),
+            jax.ShapeDtypeStruct((nodes, *share), bf16),
+            jax.ShapeDtypeStruct((8, 128), f32),
+        ],
+        scratch_shapes=[
+            pltpu.VMEM((8 * world, width), f32),
+            pltpu.VMEM((world, 8, width), f32),
+            pltpu.VMEM((world, 8, width), f32),
+            pltpu.VMEM((8, width + 128), f32),
+            pltpu.VMEM((world, 8, width + 128), f32),
+            pltpu.VMEM((nodes, *share), bf16),
+            pltpu.VMEM((nodes, *share), bf16),
+            pltpu.SemaphoreType.DMA((8, world)),
+        ],
+        compiler_params=pltpu.CompilerParams(
+            vmem_limit_bytes=48 * MIB, collective_id=1, has_side_effects=True
+        ),
+        name="settle",
+    )(feat_sq, d_norm, h_zero, d_one, node_in, modulation, grad_dec, gmod_two, grad_qkv, big_share, loss)
 
 
 def eliminate(blocks):
@@ -762,14 +907,15 @@
     from_above = passed_along(kv_low, "node", -1)
     from_below = passed_along(kv_high, "node", 1)
     dn_part, grad_qkv = unproject(dq, kv_self, from_below, from_above, norm_all, w_attn, 512)
-    qkv_share = lax.psum_scatter(grad_qkv, "node", scatter_dimension=0, tiled=True)
     d_norm = lax.all_to_all(dn_part.reshape(heads, rows, width), "head", 0, 0)
-    grad_enc, gmod_one = leave(d_norm, h_zero, d_one, node_in, modulation)
-
-    grad_enc = jnp.concatenate([grad_enc[:VARS], grad_enc[SLOT : SLOT + VARS]], 0)
-    d_mod = jnp.concatenate([gmod_one[:2], gmod_two[:2]], 0)
-    grad_enc, d_mod, grad_dec = lax.psum((grad_enc, d_mod, grad_dec[:VARS]), both)
-    grad_cond = noise_feat[:, None] * d_mod.reshape(1, -1)
+    feat_sq = jnp.sum(noise_feat * noise_feat).reshape(1)
+    small, qkv_share, qkv_full, sums = settle(
+        feat_sq, d_norm, h_zero, d_one, node_in, modulation, grad_dec, gmod_two, grad_qkv, big_share,
+        loss_part, groups,
+    )
+    grad_enc = small[: 2 * VARS]
+    grad_dec = small[2 * VARS : 3 * VARS]
+    grad_cond = noise_feat[:, None] * small[3 * VARS : 3 * VARS + 4].reshape(1, -1)
     layer_share = jnp.stack(
         [
             jnp.concatenate([qkv_share, big_share[:, 2 * width :]], 1),
@@ -777,15 +923,19 @@
             big_share[:, width : 2 * width],
         ]
     )
-    small_sq = (
-        jnp.sum(grad_enc * grad_enc) + jnp.sum(grad_cond * grad_cond) + jnp.sum(grad_dec * grad_dec)
-    )
-    total_sq, loss_sum = lax.psum((jnp.sum(layer_share * layer_share), jnp.sum(loss_part[:VARS])), both)
-    grad_norm = jnp.sqrt(total_sq + small_sq)
+    grad_norm = jnp.sqrt(sums[0, 0])
+    loss_sum = sums[1, 0]
     clip_factor = clip_limit / jnp.maximum(grad_norm, clip_limit)
     clipped = clip_factor * layer_share
-    grad_full = lax.all_gather(layer_share, "node", axis=1, tiled=True)
-    raw_stat = jnp.einsum("idb,idc->ibc", grad_full, grad_full, precision=highest)
+    big_full = lax.all_gather(big_share.astype(bf16), "node", axis=0, tiled=True)
+    grad_full = jnp.stack(
+        [
+            jnp.concatenate([qkv_full.reshape(width, -1), big_full[:, 2 * width :]], 1),
+            big_full[:, :width],
+            big_full[:, width : 2 * width],
+        ]
+    )
+    raw_stat = jnp.einsum("idb,idc->ibc", grad_full, grad_full, preferred_element_type=f32)
     stat_new = clip_factor * (clip_factor * raw_stat)
     basis_old = soap_basis[:, 0]
     rotated = jnp.einsum("idb,ibc->idc", clipped, basis_old, precision=highest)

time: 763 us -> 617 us (0.81)
  waiting for transfers between devices: 279 us -> 113 us
  Pallas kernels: 229 us -> 278 us
  blocking collectives: 135 us -> 123 us
  matrix products: 27.1 us -> 19.1 us
    psum x1 -> x0, waiting for transfers between devices: 128 us -> none  [local(): lax.psum((grad_enc, d_mod, grad_dec[:VARS]), both)]
    pallas_call x1, Pallas kernels: 3.46 us -> 52.9 us  [settle(): pl.pallas_call(settle_kernel, in_specs=[smem()] + [pl.BlockSpec(memory_sp...]
    psum x1 -> x0, blocking collectives: 41.3 us -> none  [local(): lax.psum((jnp.sum(layer_share * layer_share), jnp.sum(loss_part[:VARS])),...]
    all_to_all x1 -> x0, waiting for transfers between devices: 32.2 us -> none  [local(): d_norm = lax.all_to_all(dn_part.reshape(heads, rows, width), 'head', 0, 0)]
    reduce_scatter x1 -> x0, waiting for transfers between devices: 30.9 us -> none  [local(): lax.psum_scatter(grad_qkv, 'node', scatter_dimension=0, tiled=True)]
    all_to_all x0 -> x1, blocking collectives: none -> 29.3 us  [local(): d_norm = lax.all_to_all(dn_part.reshape(heads, rows, width), 'head', 0, 0)]
    reduce_scatter x1, waiting for transfers between devices: 22.2 us -> 38.2 us  [local(): lax.psum_scatter(grad_big.reshape(heads * width, -1), both, scatter_dimen...]
    all_gather x1, waiting for transfers between devices: 0.01 us -> 9.22 us  [local(): lax.all_gather(big_share.astype(bf16), 'node', axis=0, tiled=True)]
  transfers between devices with their start and end apart: 12 -> 9, of which waited for: 8 -> 6; matrix products, arithmetic and copies ran while one was open for 4% -> 4% of each run, Pallas kernels for 13% -> 16%
where the time goes in v2:
time: 617 us; the launch traced here: 607 us
  Pallas kernels  278 us (45%)
  blocking collectives  123 us (20%)
  waiting for transfers between devices  113 us (18%)
  local copies, waits for them, and re-layouts  29.7 us (5%)
  between operations  19.8 us (3%)
  matrix products  19.1 us (3%)
  other arithmetic  13.5 us (2%)
  starting transfers between devices  11.4 us (2%)
    pallas_call x1, Pallas kernels, renew(): pl.pallas_call(renew_kernel, grid=(size // BLOCK,), in_specs=[whole(gram....  75.1 us
    pallas_call x1, Pallas kernels, settle(): pl.pallas_call(settle_kernel, in_specs=[smem()] + [pl.BlockSpec(memory_sp...  52.9 us
    ppermute x4, waiting for transfers between devices, passed_along(): lax.ppermute(x, axis, [(i, (i + by) % length) for i in range(length)])  42.4 us
    psum x1, blocking collectives, local(): stat_sum = lax.psum(jnp.sum(stat, 1), 'node')  39.7 us
    reduce_scatter x1, waiting for transfers between devices, local(): lax.psum_scatter(grad_big.reshape(heads * width, -1), both, scatter_dimen...  38.2 us
    pallas_call x1, Pallas kernels, attend_back(): pl.pallas_call(functools.partial(attend_back_kernel, chunk=chunk), grid=(...  36.6 us
    pallas_call x1, Pallas kernels, attend(): pl.pallas_call(functools.partial(attend_kernel, chunk=chunk), grid=(nodes...  35.7 us
    all_to_all x1, blocking collectives, local(): d_norm = lax.all_to_all(dn_part.reshape(heads, rows, width), 'head', 0, 0)  29.3 us
  transfers between devices with their start and end apart: 9, of which 6 were waited for; matrix products, arithmetic and copies ran while one was open for 4% of the time, Pallas kernels for 16%

profile of v2, /device:TPU:0, one launch (start us, length us, event | category | flops | bytes accessed | tf_op | source)
XLA Modules:
  0.0 607.2 jit_solution(7058035524776679012)
XLA Ops:
  15.0 10.7 %encode.1 = (f32[512,256]{1,0:T(8,128)S(1)}, f32[96,128]{1,0:T(8,128)S(1)}) custom-call(s32[4]{0:T(128)S(1)} %pad_add_fusion.place_ref, f32[2]{0:T(128)S(1)} %pad_maximum_fusion.2.scale_ref, s32[1,12288]{1,0:T(1,128)S(1)} %bitcast.134, f32[84,12288]{1,0:T(8,128)S(1)} %bitcast.124, f32[84,12288]{1,0:T(8,128)} %bitcast.139, f32[84,12288]{1,0:T(8,128)} %bitcast.141), custom_call_target="tpu_custom_call" | custom-call | tf_op jit(solution)/shard_map/encode/pallas_call | solution.py:149
  30.3 17.6 %all-gather = bf16[1,512,512]{2,1,0:T(8,128)(2,1)} all-gather(bf16[1,64,512]{2,1,0:T(8,128)(2,1)S(1)} %get-tuple-element.158), channel_id=2, replica_groups=mesh['head'=4,'node'=8] {'node'}, dimensions={1}, use_global_device_ids=true | all-gather | bytes 589824 | tf_op jit(solution)/shard_map/all_gather | solution.py:847
  47.9 18.8 %all-gather.6.cloned.1.call-done.norm_ref = bf16[2048,512]{1,0:T(8,128)(2,1)} async-done(((bf16[512,512]{1,0:T(8,128)(2,1)}), bf16[2048,512]{1,0:T(8,128)(2,1)}) %all-gather.6.cloned.1.call-update) | async-done | bytes 2097168 | tf_op jit(solution)/shard_map/all_gather | solution.py:874
  76.6 39.7 %psum.7 = f32[96]{0:T(128)S(1)} all-reduce(f32[96]{0:T(128)S(1)} %reduce_sum.19), channel_id=1, replica_groups=mesh['head'=4,'node'=8] {'node'}, use_global_device_ids=true, to_apply=%region_2.0 | all-reduce | flops 96 | bytes 768 | tf_op jit(solution)/shard_map/psum | solution.py:866
  120.8 14.9 %count_slots.1.count_ref = bf16[2048,6144]{1,0:T(8,128)(2,1)} custom-call(s32[128,256]{1,0:T(8,128)S(1)} %reshape.163.slot_ref), custom_call_target="tpu_custom_call" | custom-call | tf_op jit(solution)/shard_map/count_slots/pallas_call | solution.py:234
  135.7 35.7 %attend.1 = (bf16[2048,6144]{1,0:T(8,128)(2,1)}, f32[2048,256]{1,0:T(8,128)}, bf16[2048,128]{1,0:T(8,128)(2,1)}) custom-call(bf16[2048,128]{1,0:T(8,128)(2,1)} %copy-done.10, bf16[2048,256]{1,0:T(8,128)(2,1)} %collective-permute-done.below_ref, bf16[2048,256]{1,0:T(8,128)(2,1)} %get-tuple-element.77.here_ref, ...), custom_call_target="tpu_custom_call" | custom-call | tf_op jit(solution)/shard_map/attend/pallas_call | solution.py:279
  178.0 4.2 all-to-all-done.mixed_ref
  183.5 9.4 %forward.1 = (f32[512,512]{1,0:T(8,128)S(1)}, f32[512,512]{1,0:T(8,128)S(1)}, bf16[512,512]{1,0:T(8,128)(2,1)S(1)}, f32[4,512,512]{2,1,0:T(8,128)}, bf16[4,512,5...) custom-call(bf16[4,512,128]{2,1,0:T(8,128)(2,1)} %all-to-all-done.mixed_ref, f32[512,512]{1,0:T(8,128)S(1)} %copy-done.6, ...), custom_call_target="tpu_custom_call" | custom-call | tf_op jit(solution)/shard_map/forward/pallas_call | solution.py:383
  194.9 11.7 %all-gather.1 = bf16[768,512]{1,0:T(8,128)(2,1)S(1)} all-gather(bf16[192,512]{1,0:T(8,128)(2,1)S(1)} %get-tuple-element.80), channel_id=3, replica_groups=mesh['head'=4,'node'=8] {'head'}, dimensions={0}, use_global_device_ids=true | all-gather | bytes 983040 | tf_op jit(solution)/shard_map/all_gather | solution.py:888
  206.7 16.7 %pixels_back.1 = (f32[96,128]{1,0:T(8,128)S(1)}, f32[2048,128]{1,0:T(8,128)S(1)}) custom-call(s32[4]{0:T(128)S(1)} %pad_add_fusion.place_ref, f32[5]{0:T(128)S(1)} %stack.66.scale_ref, s32[1,12288]{1,0:T(1,128)S(1)} %bitcast.135, s32[3,12288]{1,0:T(4,128)S(1)} %bitcast.136, f32[84,12288]{1,0:T(8,128)} %bitcast.140, f32[84,12288]{1,0:T(8,128)} %bitcast.142, ...), custom_call_target="tpu_custom_call" | custom-call | tf_op jit(solution)/shard_map/pixels_back/pallas_call | solution.py:442
  223.4 13.5 %all_to_all.20.d_ref = f32[4,512,128]{2,1,0:T(8,128)} all-to-all(f32[4,512,128]{2,1,0:T(8,128)S(1)} %bitcast.128), channel_id=1, replica_groups=mesh['head'=4,'node'=8] {'head'}, dimensions={0} | all-to-all | bytes 2097152 | tf_op jit(solution)/shard_map/all_to_all | solution.py:896
  236.9 17.0 %backward.1 = (f32[512,512]{1,0:T(8,128)}, bf16[4,512,128]{2,1,0:T(8,128)(2,1)}, f32[4,512,1152]{2,1,0:T(8,128)}, f32[96,512]{1,0:T(8,128)}, f32[8,512]{1,0:T(8,128)}) custom-call(f32[4,512,128]{2,1,0:T(8,128)} %all_to_all.20.d_ref, f32[512,512]{1,0:T(8,128)} %copy-done.15, f32[512,512]{1,0:T(8,128)} %copy-done.14, bf16[512,512]{1,0:T(8,128)(2,1)} %copy-done.21, ...), custom_call_target="tpu_custom_call" | custom-call | tf_op jit(solution)/shard_map/backward/pallas_call | solution.py:518
  254.0 11.3 %all_to_all.21 = bf16[4,512,128]{2,1,0:T(8,128)(2,1)} all-to-all(bf16[4,512,128]{2,1,0:T(8,128)(2,1)} %get-tuple-element.87), channel_id=1, replica_groups=mesh['head'=4,'node'=8] {'head'}, dimensions={0} | all-to-all | bytes 1048576 | tf_op jit(solution)/shard_map/all_to_all | solution.py:903
  265.3 36.6 %attend_back.1 = (bf16[2048,128]{1,0:T(8,128)(2,1)}, bf16[256,2048]{1,0:T(8,128)(2,1)}, f32[256,2048]{1,0:T(8,128)}, bf16[256,2048]{1,0:T(8,128)(2,1)}) custom-call(bf16[2048,128]{1,0:T(8,128)(2,1)} %copy-done.10, bf16[2048,128]{1,0:T(8,128)(2,1)} %bitcast.146, f32[2048,256]{1,0:T(8,128)} %get-tuple-element.88.mix_ref, ...), custom_call_target="tpu_custom_call" | custom-call | tf_op jit(solution)/shard_map/attend_back/pallas_call | solution.py:338
  305.5 36.3 %collective-permute-done.2.down_ref = bf16[256,2048]{1,0:T(8,128)(2,1)S(1)} collective-permute-done((bf16[256,2048]{1,0:T(8,128)(2,1)}, bf16[256,2048]{1,0:T(8,128)(2,1)S(1)}, u32[]{:S(2)}, u32[]{:S(2)}) %collective-permute-start.2) | collective-permute-done | bytes 1048608 | tf_op jit(solution)/shard_map/ppermute | solution.py:41
  341.8 6.1 %collective-permute-done.3.up_ref = bf16[256,2048]{1,0:T(8,128)(2,1)S(1)} collective-permute-done((bf16[256,2048]{1,0:T(8,128)(2,1)}, bf16[256,2048]{1,0:T(8,128)(2,1)S(1)}, u32[]{:S(2)}, u32[]{:S(2)}) %collective-permute-start.3) | collective-permute-done | bytes 1048608 | tf_op jit(solution)/shard_map/ppermute | solution.py:41
  349.0 5.0 unproject.1
  354.8 29.3 %all_to_all.22.dn_ref = bf16[4,512,512]{2,1,0:T(8,128)(2,1)} all-to-all(bf16[4,512,512]{2,1,0:T(8,128)(2,1)S(1)} %bitcast.126), channel_id=1, replica_groups=mesh['head'=4,'node'=8] {'head'}, dimensions={0} | all-to-all | bytes 4194304 | tf_op jit(solution)/shard_map/all_to_all | solution.py:910
  384.1 38.2 %reduce-scatter.2.cloned.1.call-done.big_ref = f32[64,1152]{1,0:T(8,128)} async-done(((f32[2048,1152]{1,0:T(8,128)}), f32[64,1152]{1,0:T(8,128)}) %reduce-scatter.2.cloned.1.call-update) | async-done | bytes 294928 | tf_op jit(solution)/shard_map/reduce_scatter | solution.py:900
  428.8 52.9 %settle.1 = (f32[256,512]{1,0:T(8,128)S(1)}, f32[64,384]{1,0:T(8,128)S(1)}, bf16[8,64,384]{2,1,0:T(8,128)(2,1)S(1)}, f32[8,128]{1,0:T(8,128)S(1)}) custom-call(f32[1]{0:T(128)} %bitcast.1.feat_ref, bf16[4,512,512]{2,1,0:T(8,128)(2,1)} %all_to_all.22.dn_ref, f32[512,512]{1,0:T(8,128)S(1)} %copy-done.7, f32[512,512]{1,0:T(8,128)S(1)} %copy-done.13, ...), custom_call_target="tpu_custom_call" | custom-call | tf_op jit(solution)/shard_map/settle/pallas_call | solution.py:719
  499.4 9.2 %all-gather.10.cloned.1.call-done = bf16[512,1152]{1,0:T(8,128)(2,1)} async-done(((bf16[64,1152]{1,0:T(8,128)(2,1)}), bf16[512,1152]{1,0:T(8,128)(2,1)}) %all-gather.10.cloned.1.call-update) | async-done | bytes 1179664 | tf_op jit(solution)/shard_map/all_gather | solution.py:930
  512.4 5.3 fusion.product_ref
  517.7 5.4 fusion.58.gram_ref
  523.1 75.1 %renew.1 = f32[3,512,512]{2,1,0:T(8,128)} custom-call(f32[3,512,512]{2,1,0:T(8,128)S(1)} %fusion.58.gram_ref, f32[3,512,512]{2,1,0:T(8,128)} %copy-done.33), custom_call_target="tpu_custom_call" | custom-call | tf_op jit(solution)/shard_map/renew/pallas_call | solution.py:799
  (148 shorter events, 66.7 us)
Async XLA Ops:
  7.2 485.1 %copy-start = (f32[3,1,512,512]{3,2,1,0:T(8,128)S(1)}, f32[3,1,512,512]{3,2,1,0:T(8,128)}, u32[]{:S(2)}) copy-start(f32[3,1,512,512]{3,2,1,0:T(8,128)} %param.42) | copy-start | bytes 9437188
  7.2 59.4 %all-gather.6.cloned.1.call-start = ((), (), s32[]{:S(2)}) async-start(), calls=%async_computation.5 | async-start | bytes 2621440 | tf_op jit(solution)/shard_map/all_gather | solution.py:874
  11.9 170.4 %copy-start.25 = (f32[1,4,512]{2,1,0:T(4,128)}, f32[1,4,512]{2,1,0:T(4,128)S(1)}, u32[]{:S(2)}) copy-start(f32[1,4,512]{2,1,0:T(4,128)S(1)} %copy.63) | copy-start | bytes 24580
  25.8 91.1 %copy-start.43 = (s32[2048]{0:T(1024)S(1)}, s32[2048]{0:T(1024)}, u32[]{:S(2)}) copy-start(s32[2048]{0:T(1024)} %param.33) | copy-start | bytes 24580
  28.5 153.8 %all-gather.8.cloned.1.call-start = ((), (), s32[]{:S(2)}) async-start(), calls=%async_computation.6 | async-start | bytes 4866048 | tf_op jit(solution)/shard_map/all_gather | solution.py:849
  72.9 62.9 %collective-permute-start = (bf16[2048,256]{1,0:T(8,128)(2,1)}, bf16[2048,256]{1,0:T(8,128)(2,1)}, u32[]{:S(2)}, u32[]{:S(2)}) collective-permute-start(bf16[2048,256]{1,0:T(8,128)(2,1)} %get-tuple-element.77.here_ref), channel_id=1, source_target_pairs={{0,1},{1,2},{2,3},{3,4},{4,5},{5,6},{6,7},{7,0},{8,9},{9,10},{10,1... | collective-permute-start | bytes 3145736 | tf_op jit(solution)/shard_map/ppermute | solution.py:41
  72.9 62.9 %collective-permute-start.1 = (bf16[2048,256]{1,0:T(8,128)(2,1)}, bf16[2048,256]{1,0:T(8,128)(2,1)}, u32[]{:S(2)}, u32[]{:S(2)}) collective-permute-start(bf16[2048,256]{1,0:T(8,128)(2,1)} %get-tuple-element.77.here_ref), channel_id=1, source_target_pairs={{0,7},{1,0},{2,1},{3,2},{4,3},{5,4},{6,5},{7,6},{8,15},{9,8},{10,9... | collective-permute-start | bytes 3145736 | tf_op jit(solution)/shard_map/ppermute | solution.py:41
  171.4 10.8 %all-to-all-start = ((bf16[4,512,128]{2,1,0:T(8,128)(2,1)}), bf16[4,512,128]{2,1,0:T(8,128)(2,1)}, u32[]{:S(2)}, u32[]{:S(2)}) async-start(bf16[4,512,128]{2,1,0:T(8,128)(2,1)} %bitcast.148), calls=%async_computation | async-start | bytes 1048576 | tf_op jit(solution)/shard_map/all_to_all | solution.py:884
  175.6 246.7 %reduce-scatter.2.cloned.1.call-start = ((), (), s32[]{:S(2)}) async-start(), calls=%async_computation.7 | async-start | bytes 9732096 | tf_op jit(solution)/shard_map/reduce_scatter | solution.py:900
  176.6 16.3 %copy-start.16 = (bf16[96,512]{1,0:T(8,128)(2,1)}, bf16[96,512]{1,0:T(8,128)(2,1)S(1)}, u32[]{:S(2)}) copy-start(bf16[96,512]{1,0:T(8,128)(2,1)S(1)} %scatter.9.wdec_ref) | copy-start | bytes 294916
  183.5 23.2 %copy-start.28 = (s32[12288]{0:T(1024)S(1)}, s32[12288]{0:T(1024)}, u32[]{:S(2)}) copy-start(s32[12288]{0:T(1024)} %param.34) | copy-start | bytes 147460
  183.5 23.2 %copy-start.30 = (s32[12288,3]{0,1:T(4,128)S(1)}, s32[12288,3]{0,1:T(4,128)}, u32[]{:S(2)}) copy-start(s32[12288,3]{0,1:T(4,128)} %param.35) | copy-start | bytes 442372
  194.9 28.5 %copy-start.21 = (bf16[512,512]{1,0:T(8,128)(2,1)}, bf16[512,512]{1,0:T(8,128)(2,1)S(1)}, u32[]{:S(2)}) copy-start(bf16[512,512]{1,0:T(8,128)(2,1)S(1)} %get-tuple-element.84.norm_ref) | copy-start | bytes 1572868
  253.9 254.7 %all-gather.10.cloned.1.call-start = ((), (), s32[]{:S(2)}) async-start(), calls=%async_computation.8 | async-start | bytes 1327104 | tf_op jit(solution)/shard_map/all_gather | solution.py:930
  265.3 82.6 %copy-start.3 = (bf16[1,512,512]{2,1,0:T(8,128)(2,1)S(1)}, bf16[1,512,512]{2,1,0:T(8,128)(2,1)}, u32[]{:S(2)}) copy-start(bf16[1,512,512]{2,1,0:T(8,128)(2,1)} %all-gather) | copy-start | bytes 1572868
  302.0 39.9 %collective-permute-start.2 = (bf16[256,2048]{1,0:T(8,128)(2,1)}, bf16[256,2048]{1,0:T(8,128)(2,1)S(1)}, u32[]{:S(2)}, u32[]{:S(2)}) collective-permute-start(bf16[256,2048]{1,0:T(8,128)(2,1)} %get-tuple-element.92), channel_id=1, source_target_pairs={{0,1},{1,2},{2,3},{3,4},{4,5},{5,6},{6,7},{7,0},{8,9},{9,10},{10,1... | collective-permute-start | bytes 3145736 | tf_op jit(solution)/shard_map/ppermute | solution.py:41
  302.0 45.9 %collective-permute-start.3 = (bf16[256,2048]{1,0:T(8,128)(2,1)}, bf16[256,2048]{1,0:T(8,128)(2,1)S(1)}, u32[]{:S(2)}, u32[]{:S(2)}) collective-permute-start(bf16[256,2048]{1,0:T(8,128)(2,1)} %get-tuple-element.93), channel_id=1, source_target_pairs={{0,7},{1,0},{2,1},{3,2},{4,3},{5,4},{6,5},{7,6},{8,15},{9,8},{10,9... | collective-permute-start | bytes 3145736 | tf_op jit(solution)/shard_map/ppermute | solution.py:41
  354.8 67.5 %copy-start.26 = (f32[1,4,512]{2,1,0:T(4,128)S(1)}, f32[1,4,512]{2,1,0:T(4,128)}, u32[]{:S(2)}) copy-start(f32[1,4,512]{2,1,0:T(4,128)} %copy-done.25) | copy-start | bytes 24580
  354.8 67.5 %copy-start.32 = (f32[8,512]{1,0:T(8,128)S(1)}, f32[8,512]{1,0:T(8,128)}, u32[]{:S(2)}) copy-start(f32[8,512]{1,0:T(8,128)} %get-tuple-element.97.gmod_ref) | copy-start | bytes 49156
  428.8 57.9 %slice-start = ((f32[64,1152]{1,0:T(8,128)}), f32[64,128]{1,0:T(8,128)S(1)}, s32[]{:S(2)}) async-start(f32[64,1152]{1,0:T(8,128)} %reduce-scatter.2.cloned.1.call-done.big_ref), calls=%async_computation.9 | async-start | bytes 65536 | tf_op jit(solution)/shard_map/slice | solution.py:921
  428.8 58.8 %copy-start.9 = (f32[64,1152]{1,0:T(8,128)S(1)}, f32[64,1152]{1,0:T(8,128)}, u32[]{:S(2)}) copy-start(f32[64,1152]{1,0:T(8,128)} %reduce-scatter.2.cloned.1.call-done.big_ref) | copy-start | bytes 884740
  485.9 6.3 %copy-start.39 = (f32[3,64,512]{2,1,0:T(8,128)S(1)}, f32[3,64,512]{2,1,0:T(8,128)}, u32[]{:S(2)}) copy-start(f32[3,64,512]{2,1,0:T(8,128)} %param.40) | copy-start | bytes 1179652
  485.9 6.3 %copy-start.40 = (f32[3,64,512]{2,1,0:T(8,128)S(1)}, f32[3,64,512]{2,1,0:T(8,128)}, u32[]{:S(2)}) copy-start(f32[3,64,512]{2,1,0:T(8,128)} %param.41) | copy-start | bytes 1179652
  494.4 15.3 %copy-start.24 = (bf16[8,64,384]{2,1,0:T(8,128)(2,1)S(1)}, bf16[8,64,384]{2,1,0:T(8,128)(2,1)}, u32[]{:S(2)}) copy-start(bf16[8,64,384]{2,1,0:T(8,128)(2,1)} %copy-done.23) | copy-start | bytes 1179652
  (31 other events, 58.2 us)
Sparse Core Ops, SparseCore 0:
  28.6 38.0 all-gather.5
  70.2 64.9 all-gather.7
  254.1 168.1 reduce-scatter.1
  486.0 22.5 all-gather.9

commit v3 on v2

--- a/solution.py
+++ b/solution.py
@@ -19,6 +19,7 @@
 SLIM = 96
 GROUP = 256 // NBR
 BLOCK = 128
+STRIP = 16
 
 highest = lax.Precision.HIGHEST
 clip_limit = 0.01
@@ -116,13 +117,81 @@
     return pltpu.CompilerParams(vmem_limit_bytes=mib * MIB)
 
 
-def encode_kernel(place_ref, scale_ref, node_ref, prev_ref, target_ref, eps_ref, in_ref, stat_ref, pix):
+def remote(mib, identity):
+    return pltpu.CompilerParams(
+        vmem_limit_bytes=mib * MIB, collective_id=identity, has_side_effects=True
+    )
+
+
+def vmem():
+    return pl.BlockSpec(memory_space=pltpu.VMEM)
+
+
+def each(count, act, start=1):
+    def body(off, carry):
+        act(off)
+        return carry
+
+    lax.fori_loop(start, count, body, 0)
+
+
+def meet(axes):
+    barrier = pltpu.get_barrier_semaphore()
+    total = 0
+    for axis in axes:
+        count, me = lax.axis_size(axis), lax.axis_index(axis)
+        total += count - 1
+        each(
+            count,
+            lambda off: pl.semaphore_signal(barrier, inc=1, device_id={axis: (me + off) % count}),
+        )
+    pl.semaphore_wait(barrier, total)
+
+
+class Spread:
+    def __init__(self, axis, source, target, sends, receives):
+        self.axis, self.source, self.target = axis, source, target
+        self.sends, self.receives = sends, receives
+        self.count, self.me = lax.axis_size(axis), lax.axis_index(axis)
+
+    def copy(self, other, slot):
+        return pltpu.make_async_remote_copy(
+            src_ref=self.source(other),
+            dst_ref=self.target(slot),
+            send_sem=self.sends.at[other],
+            recv_sem=self.receives.at[slot],
+            device_id={self.axis: other},
+        )
+
+    def other(self, off):
+        return (self.me + off) % self.count
+
+    def start(self, off):
+        self.copy(self.other(off), self.me).start()
+
+    def arrived(self, off):
+        self.copy(self.other(off), self.other(off)).wait_recv()
+
+    def sent(self, off):
+        self.copy(self.other(off), self.me).wait_send()
+
+    def all(self, act):
+        each(self.count, getattr(self, act))
+
+
+def encode_kernel(
+    place_ref, scale_ref, node_ref, prev_ref, target_ref, eps_ref, w_ref, in_ref, stat_ref, all_ref, pix, box, sems
+):
     step = pl.program_id(0)
     rows = in_ref.shape[0]
     tile = node_ref.shape[1]
+    weights = Spread("node", lambda _: w_ref, lambda i: box.at[i], sems.at[0], sems.at[1])
 
     @pl.when(step == 0)
     def _():
+        meet(["node"])
+        weights.all("start")
+        box[weights.me] = w_ref[...]
         pix[...] = jnp.zeros_like(pix)
         in_ref[...] = jnp.zeros_like(in_ref)
         stat_ref[...] = jnp.zeros_like(stat_ref)
@@ -142,108 +211,208 @@
     stat_ref[:VARS] += fold_lanes(valid * residual * residual)
     stat_ref[SLIM - 1 : SLIM] += fold_lanes(valid)
 
-
-def encode(place, scales, node_row, prev, target, eps, rows, tile):
+    @pl.when(step == pl.num_programs(0) - 1)
+    def _():
+        weights.all("arrived")
+        all_ref[...] = box[...]
+        weights.all("sent")
+
+
+def encode(place, scales, node_row, prev, target, eps, w_share, rows, tile, nodes):
     pixels = prev.shape[1]
+    gathered = (nodes, *w_share.shape)
     pixel_block = pl.BlockSpec((VARS, tile), lambda i: (0, i))
     return pl.pallas_call(
         encode_kernel,
         grid=(pixels // tile,),
-        in_specs=[smem(), smem(), pl.BlockSpec((1, tile), lambda i: (0, i))] + [pixel_block] * 3,
-        out_specs=[whole((rows, 2 * SLOT)), whole((SLIM, 128))],
+        in_specs=[smem(), smem(), pl.BlockSpec((1, tile), lambda i: (0, i))]
+        + [pixel_block] * 3
+        + [whole(w_share.shape)],
+        out_specs=[whole((rows, 2 * SLOT)), whole((SLIM, 128)), whole(gathered)],
         out_shape=[
             jax.ShapeDtypeStruct((rows, 2 * SLOT), f32),
             jax.ShapeDtypeStruct((SLIM, 128), f32),
-        ],
-        scratch_shapes=[pltpu.VMEM((2 * SLOT, tile), bf16)],
-        compiler_params=params(),
+            jax.ShapeDtypeStruct(gathered, bf16),
+        ],
+        scratch_shapes=[
+            pltpu.VMEM((2 * SLOT, tile), bf16),
+            pltpu.VMEM(gathered, bf16),
+            pltpu.SemaphoreType.DMA((2, nodes)),
+        ],
+        compiler_params=remote(48, 2),
         name="encode",
-    )(place, scales, node_row, prev, target, eps)
-
-
-def enter_kernel(in_ref, w_ref, mod_ref, zero_ref, norm_ref):
-    w = w_ref[...]
-    h_zero = sum(contract(part, w, 1, 0) for part in thirds(in_ref[...]))
-    zero_ref[...] = h_zero
-    normed, _ = standardize(h_zero)
-    norm_ref[...] = (normed * (1 + mod_ref[0:1]) + mod_ref[1:2]).astype(bf16)
-
-
-def enter(node_in, w_enc, modulation):
-    rows, width = node_in.shape[0], w_enc.shape[1]
-    return pl.pallas_call(
-        enter_kernel,
-        out_shape=[
-            jax.ShapeDtypeStruct((rows, width), f32),
-            jax.ShapeDtypeStruct((rows, width), bf16),
-        ],
-        compiler_params=params(),
-        name="enter",
-    )(node_in, w_enc, modulation)
-
-
-def project_kernel(norm_ref, w_ref, q_ref, kv_ref):
-    out = contract(norm_ref[...], w_ref[...], 1, 0).astype(bf16)
-    q_ref[...] = out[:, :HD]
-    kv_ref[...] = out[:, HD : 3 * HD]
-
-
-def project(norm_all, w_attn, tile):
-    nodes, width = norm_all.shape
-    return pl.pallas_call(
-        project_kernel,
-        grid=(nodes // tile,),
-        in_specs=[
-            pl.BlockSpec((tile, width), lambda i: (i, 0)),
-            pl.BlockSpec((width, 3 * HD), lambda i: (0, 0)),
-        ],
-        out_specs=[
-            pl.BlockSpec((tile, HD), lambda i: (i, 0)),
-            pl.BlockSpec((tile, 2 * HD), lambda i: (i, 0)),
-        ],
-        out_shape=[
-            jax.ShapeDtypeStruct((nodes, HD), bf16),
-            jax.ShapeDtypeStruct((nodes, 2 * HD), bf16),
-        ],
-        compiler_params=params(),
-        name="project",
-    )(norm_all, w_attn)
-
-
-def count_kernel(slot_ref, count_ref):
-    groups = slot_ref.shape[0]
-    bands = count_ref.shape[1] // 256
+    )(place, scales, node_row, prev, target, eps, w_share)
+
+
+def count_tile(slots, put, bands):
     lane = lax.broadcasted_iota(jnp.int32, (GROUP, 256), 1)
     sub = lax.broadcasted_iota(jnp.int32, (GROUP, 256), 0)
     own = lane // NBR == sub
     spot = lax.broadcasted_iota(jnp.int32, (256, 256), 0)
-    for g in range(groups):
-        row = slot_ref[g : g + 1]
+    for g in range(slots.shape[0]):
+        row = slots[g : g + 1]
         band = jnp.where(own, row >> 8, -1)
         left = jnp.concatenate([(band == t).astype(f32).astype(bf16) for t in range(bands)], 0)
         right = (spot == (row & 255)).astype(f32).astype(bf16)
         found = contract(left, right, 1, 1).astype(bf16)
         for t in range(bands):
-            count_ref[g * GROUP : (g + 1) * GROUP, t * 256 : (t + 1) * 256] = found[
-                t * GROUP : (t + 1) * GROUP
-            ]
-
-
-def count_slots(slots, reach, tile_groups):
-    groups = slots.shape[0]
+            put(g, t, found[t * GROUP : (t + 1) * GROUP])
+
+
+def open_kernel(
+    in_ref, wenc_ref, mod_ref, stat_ref, w_ref, slot_ref,
+    zero_ref, norm_ref, q_ref, here_ref, below_ref, above_ref, sum_ref, count_ref,
+    norm_box, stat_own, stat_box, kv, low_box, high_box, tiles, head_sems, stat_sems, halo_sems, out_sems,
+):
+    heads, rows, _ = norm_box.shape
+    head, node = lax.axis_index("head"), lax.axis_index("node")
+    nodes = lax.axis_size("node")
+    depth = tiles.shape[1]
+    steps = count_ref.shape[0] // depth
+    stat_own[...] = jnp.broadcast_to(
+        jnp.sum(stat_ref[...], 1, keepdims=True), stat_own.shape
+    )
+    meet(["head", "node"])
+
+    stats = Spread("node", lambda _: stat_own, lambda i: stat_box.at[i], stat_sems.at[0], stat_sems.at[1])
+    stats.all("start")
+    w_enc = wenc_ref[...]
+    h_zero = sum(contract(part, w_enc, 1, 0) for part in thirds(in_ref[...]))
+    zero_ref[...] = h_zero
+    normed, _ = standardize(h_zero)
+    norm_box[head] = (normed * (1 + mod_ref[0:1]) + mod_ref[1:2]).astype(bf16)
+    norms = Spread(
+        "head", lambda _: norm_box.at[head], lambda i: norm_box.at[i], head_sems.at[0], head_sems.at[1]
+    )
+    norms.all("start")
+
+    def halo(block):
+        return [
+            pltpu.make_async_remote_copy(
+                src_ref=kv.at[block],
+                dst_ref=box.at[block],
+                send_sem=halo_sems.at[2 * side, block],
+                recv_sem=halo_sems.at[2 * side + 1, block],
+                device_id={"node": (node + by) % nodes},
+            )
+            for side, (box, by) in enumerate(((low_box, 1), (high_box, nodes - 1)))
+        ]
+
+    def project(block):
+        out = contract(norm_box[block], w_ref[:, : 3 * HD], 1, 0).astype(bf16)
+        q_ref[block] = out[:, :HD]
+        kv[block] = out[:, HD:]
+        for copy in halo(block):
+            copy.start()
+
+    def count(step):
+        slot = step % 2
+
+        @pl.when(step >= 2)
+        def _():
+            count_out(step - 2).wait()
+
+        per = depth // GROUP
+        slots = slot_ref[pl.ds(pl.multiple_of(step * per, per), per)]
+
+        def put(g, t, found):
+            tiles[slot, g * GROUP : (g + 1) * GROUP, t * 256 : (t + 1) * 256] = found
+
+        count_tile(slots, put, tiles.shape[2] // 256)
+        count_out(step).start()
+
+    def count_out(step):
+        return pltpu.make_async_copy(
+            tiles.at[step % 2],
+            count_ref.at[pl.ds(pl.multiple_of(step * depth, depth), depth)],
+            out_sems.at[step % 2],
+        )
+
+    project(head)
+    each(steps // 2, count, 0)
+
+    def next_block(off):
+        norms.arrived(off)
+        project(norms.other(off))
+
+    each(heads, next_block)
+    norm_ref[...] = norm_box[...]
+    here_ref[...] = kv[...]
+    each(steps, count, steps // 2)
+    each(steps, lambda step: count_out(step).wait(), steps - 2)
+    stats.all("arrived")
+    sum_ref[...] = sum(jnp.where(t == node, stat_own[...], stat_box[t]) for t in range(nodes))
+
+    def finish(block):
+        for copy in halo(block):
+            copy.wait()
+
+    each(heads, finish, 0)
+    below_ref[...] = low_box[...]
+    above_ref[...] = high_box[...]
+    norms.all("sent")
+    stats.all("sent")
+
+
+def open_nodes(node_in, w_enc, modulation, stat, w_attn, slots, heads, groups, reach):
+    rows, width = node_in.shape[0], w_enc.shape[1]
+    depth = 8 * GROUP
+    block = lambda w: jax.ShapeDtypeStruct((heads, rows, w), bf16)
     return pl.pallas_call(
-        count_kernel,
-        grid=(groups // tile_groups,),
-        in_specs=[pl.BlockSpec((tile_groups, 256), lambda i: (i, 0))],
-        out_specs=pl.BlockSpec((tile_groups * GROUP, reach), lambda i: (i, 0)),
-        out_shape=jax.ShapeDtypeStruct((groups * GROUP, reach), bf16),
-        compiler_params=params(),
-        name="count_slots",
-    )(slots)
-
-
-def attend_kernel(q_ref, below_ref, here_ref, above_ref, count_ref, e_ref, mix_ref, low_ref, s_scr, chunk):
+        open_kernel,
+        in_specs=[vmem()] * 6,
+        out_specs=[vmem()] * 7 + [pl.BlockSpec(memory_space=pl.ANY)],
+        out_shape=[
+            jax.ShapeDtypeStruct((rows, width), f32),
+            block(width),
+            block(HD),
+            block(2 * HD),
+            block(2 * HD),
+            block(2 * HD),
+            jax.ShapeDtypeStruct((SLIM, 128), f32),
+            jax.ShapeDtypeStruct((heads * rows, reach), bf16),
+        ],
+        scratch_shapes=[
+            pltpu.VMEM((heads, rows, width), bf16),
+            pltpu.VMEM((SLIM, 128), f32),
+            pltpu.VMEM((groups, SLIM, 128), f32),
+            pltpu.VMEM((heads, rows, 2 * HD), bf16),
+            pltpu.VMEM((heads, rows, 2 * HD), bf16),
+            pltpu.VMEM((heads, rows, 2 * HD), bf16),
+            pltpu.VMEM((2, depth, reach), bf16),
+            pltpu.SemaphoreType.DMA((2, heads)),
+            pltpu.SemaphoreType.DMA((2, groups)),
+            pltpu.SemaphoreType.DMA((4, heads)),
+            pltpu.SemaphoreType.DMA((2,)),
+        ],
+        compiler_params=remote(56, 3),
+        name="open_nodes",
+    )(node_in, w_enc, modulation, stat, w_attn, slots)
+
+
+def attend_kernel(
+    q_ref, below_ref, here_ref, above_ref, count_ref, e_ref, mix_ref, out_ref, s_scr, own, box, sems, chunk
+):
+    step = pl.program_id(0)
+    steps = pl.num_programs(0)
+    head = lax.axis_index("head")
     tile = q_ref.shape[0]
+    per = box.shape[1] // tile
+
+    def copy(target, source, part):
+        at = pl.ds(pl.multiple_of(part * tile, tile), tile)
+        return pltpu.make_async_remote_copy(
+            src_ref=own.at[target, at],
+            dst_ref=box.at[source, at],
+            send_sem=sems.at[0, target, part],
+            recv_sem=sems.at[1, source, part],
+            device_id={"head": target},
+        )
+
+    @pl.when(step == 0)
+    def _():
+        meet(["head"])
+
     nodes = here_ref.shape[0]
     q = q_ref[...]
     top = jnp.full((tile, 128), -1e30, f32)
@@ -270,24 +439,54 @@
     mixed = mixed * inverse
     mix_ref[:, :HD] = mixed
     mix_ref[:, HD:] = jnp.broadcast_to(inverse, (tile, HD))
-    low_ref[...] = mixed.astype(bf16)
-
-
-def attend(query, below, here, above, counts, tile, chunk):
+    target, part = step // per, step % per
+    at = pl.ds(pl.multiple_of(part * tile, tile), tile)
+    low = mixed.astype(bf16)
+    own[target, at] = low
+
+    @pl.when(target == head)
+    def _():
+        box[head, at] = low
+
+    @pl.when(target != head)
+    def _():
+        copy(target, head, part).start()
+
+    @pl.when(step == steps - 1)
+    def _():
+        heads = box.shape[0]
+
+        def finish(off):
+            other = (head + off) % heads
+            for p in range(per):
+                copy(other, other, p).wait_recv()
+                copy(other, head, p).wait_send()
+
+        each(heads, finish)
+        out_ref[...] = box[...]
+
+
+def attend(query, below, here, above, counts, heads, tile, chunk):
     nodes, reach = counts.shape
+    rows = nodes // heads
     row = lambda width: pl.BlockSpec((tile, width), lambda i: (i, 0))
     return pl.pallas_call(
         functools.partial(attend_kernel, chunk=chunk),
         grid=(nodes // tile,),
         in_specs=[row(HD)] + [whole((nodes, 2 * HD))] * 3 + [row(reach)],
-        out_specs=[row(reach), row(2 * HD), row(HD)],
+        out_specs=[row(reach), row(2 * HD), whole((heads, rows, HD))],
         out_shape=[
             jax.ShapeDtypeStruct((nodes, reach), bf16),
             jax.ShapeDtypeStruct((nodes, 2 * HD), f32),
-            jax.ShapeDtypeStruct((nodes, HD), bf16),
-        ],
-        scratch_shapes=[pltpu.VMEM((tile, reach), f32)],
-        compiler_params=params(60),
+            jax.ShapeDtypeStruct((heads, rows, HD), bf16),
+        ],
+        scratch_shapes=[
+            pltpu.VMEM((tile, reach), f32),
+            pltpu.VMEM((heads, rows, HD), bf16),
+            pltpu.VMEM((heads, rows, HD), bf16),
+            pltpu.SemaphoreType.DMA((2, heads, rows // tile)),
+        ],
+        compiler_params=remote(60, 4),
         name="attend",
     )(query, below, here, above, counts)
 
@@ -743,55 +942,70 @@
     )(feat_sq, d_norm, h_zero, d_one, node_in, modulation, grad_dec, gmod_two, grad_qkv, big_share, loss)
 
 
-def eliminate(blocks):
-    size = blocks[0].shape[0]
-    tiles = [[b[8 * i : 8 * i + 8] for i in range(size // 8)] for b in blocks]
-    lane = lax.broadcasted_iota(jnp.int32, (8, size), 1)
-    sub = lax.broadcasted_iota(jnp.int32, (8, size), 0)
-    pivots = [jnp.zeros((1, size), f32) for _ in blocks]
-    for j in range(size):
-        first, inside = divmod(j, 8)
-        for m in range(len(blocks)):
-            row = tiles[m][first][inside : inside + 1]
-            pivot = row[:, j : j + 1]
-            here = lane[:1] == j
-            pivots[m] = jnp.where(here, pivot, pivots[m])
-            scaled = jnp.where(here, 1.0, row) * (1.0 / pivot)
-            for i in range(first, size // 8):
-                old = tiles[m][i]
-                new = jnp.where(lane == j, 0.0, old) - old[:, j : j + 1] * scaled
-                if i == first:
-                    new = jnp.where(
-                        sub > inside, new, jnp.where((sub == inside) & (lane == j), 1.0, old)
-                    )
-                tiles[m][i] = new
-    return [jnp.concatenate(t, 0) for t in tiles], pivots
-
-
-def renew_kernel(gram_ref, product_ref, out_ref, both):
+def eliminate(work, done):
+    count = work.shape[0]
+    lane = lax.broadcasted_iota(jnp.int32, (1, BLOCK), 1)
+    sub = lax.broadcasted_iota(jnp.int32, (STRIP, BLOCK), 0)
+    pivots = [jnp.ones((1, BLOCK), f32) for _ in range(count)]
+    both = lambda x: jnp.concatenate([x, x], 1)
+    for at in range(0, BLOCK, STRIP):
+        strip = slice(at, at + STRIP)
+        rows = [work[m, strip] for m in range(count)]
+        columns = [
+            [jnp.broadcast_to(rows[m][:, at + k : at + k + 1], (STRIP, BLOCK)) for k in range(STRIP)]
+            for m in range(count)
+        ]
+        scale = [jnp.ones((STRIP, BLOCK), f32) for _ in range(count)]
+        for r in range(STRIP):
+            for m in range(count):
+                column = columns[m][r]
+                pivot = jnp.broadcast_to(column[r : r + 1], (STRIP, BLOCK))
+                factor = jnp.where(sub > r, column * (1.0 / pivot), 0.0)
+                scale[m] = jnp.where(sub == r, pivot, scale[m])
+                for k in range(r + 1, STRIP):
+                    columns[m][k] = columns[m][k] - factor * columns[m][k][r : r + 1]
+                pivots[m] = jnp.where(lane == at + r, pivot[:1], pivots[m])
+                rows[m] = rows[m] - both(factor) * rows[m][r : r + 1]
+        for m in range(count):
+            done[m, strip] = rows[m][:, BLOCK:]
+            if at + STRIP < BLOCK:
+                high, mid, low = thirds(rows[m] * both(lax.rsqrt(scale[m])))
+                left = jnp.concatenate([high, high, mid, mid, high, low], 0)[:, :BLOCK]
+                right = jnp.concatenate([high, mid, high, mid, low, high], 0)
+                rest = slice(at + STRIP, BLOCK)
+                work[m, rest] -= contract(left, right, 0, 0)[rest]
+    return pivots
+
+
+def renew_kernel(gram_ref, product_ref, out_ref, gram, both, work, done):
     count, size = gram_ref.shape[:2]
     k = pl.program_id(0)
 
     @pl.when(k == 0)
     def _():
-        both[:, :size] = gram_ref[...]
-        both[:, size:] = product_ref[...]
+        gram[...] = gram_ref[...]
+        both[...] = product_ref[...]
 
     at = pl.ds(pl.multiple_of(k * BLOCK, BLOCK), BLOCK)
-    factors, pivots = eliminate([both[m, at, at] for m in range(count)])
-    below = lax.broadcasted_iota(jnp.int32, (size, BLOCK), 0) >= (k + 1) * BLOCK
-    lower = lax.broadcasted_iota(jnp.int32, (BLOCK, BLOCK), 1) <= lax.broadcasted_iota(
-        jnp.int32, (BLOCK, BLOCK), 0
+    unit = lax.broadcasted_iota(jnp.int32, (BLOCK, BLOCK), 0) == lax.broadcasted_iota(
+        jnp.int32, (BLOCK, BLOCK), 1
     )
     for m in range(count):
-        factor = jnp.where(lower, factors[m], 0.0)
-        panel = contract(both[m, :, at], factor, 1, 1, highest) * lax.rsqrt(pivots[m])
-        out_ref[m] = panel[size:]
-
-        @pl.when(k < size // BLOCK - 1)
-        def _():
-            left = jnp.where(below, panel[:size], 0.0)
-            both[m] -= contract(jnp.concatenate([left, panel[size:]], 0), left, 1, 1, highest)
+        work[m, :, :BLOCK] = gram[m, at, at]
+        work[m, :, BLOCK:] = unit.astype(f32)
+    roots = [lax.rsqrt(p) for p in eliminate(work, done)]
+    for step in range(size // BLOCK):
+
+        @pl.when(k == step)
+        def _(here=slice(step * BLOCK, (step + 1) * BLOCK), rest=(step + 1) * BLOCK):
+            for m in range(count):
+                factor = done[m]
+                panel = contract(both[m, :, here], factor, 1, 1, highest) * roots[m]
+                out_ref[m] = panel
+                if rest < size:
+                    left = contract(gram[m, rest:, here], factor, 1, 1, highest) * roots[m]
+                    both[m, :, rest:] -= contract(panel, left, 1, 1, highest)
+                    gram[m, rest:, rest:] -= contract(left, left, 1, 1, highest)
 
 
 def renew(gram, product):
@@ -802,7 +1016,12 @@
         in_specs=[whole(gram.shape), whole(gram.shape)],
         out_specs=pl.BlockSpec((count, size, BLOCK), lambda k: (0, 0, k)),
         out_shape=jax.ShapeDtypeStruct(gram.shape, f32),
-        scratch_shapes=[pltpu.VMEM((count, 2 * size, size), f32)],
+        scratch_shapes=[
+            pltpu.VMEM((count, size, size), f32),
+            pltpu.VMEM((count, size, size), f32),
+            pltpu.VMEM((count, BLOCK, 2 * BLOCK), f32),
+            pltpu.VMEM((count, BLOCK, BLOCK), f32),
+        ],
         compiler_params=params(),
         name="renew",
     )(gram, product)
@@ -844,7 +1063,6 @@
     both = ("head", "node")
 
     low_w = layer_w.astype(bf16)
-    w_attn = lax.all_gather(low_w[0], "node", axis=0, tiled=True)
     big_share = jnp.concatenate([low_w[1], low_w[2], low_w[0, :, 3 * HD :]], 1)
     w_big = lax.all_gather(big_share, both, axis=0, tiled=True).reshape(heads, width, -1)
 
@@ -860,28 +1078,27 @@
     node_row = pix_node.reshape(1, -1)
     read_rows = pix_read.T
     place = jnp.stack([block_start, quarter * rows, valid_count[0], quarter]).astype(jnp.int32)
-    node_in, stat = encode(
-        place, jnp.stack([noise_sigma, input_scale]), node_row, prev_t, target_t, eps_t, rows, 1024
-    )
-    stat_sum = lax.psum(jnp.sum(stat, 1), "node")
+    node_in, stat, w_attn = encode(
+        place, jnp.stack([noise_sigma, input_scale]), node_row, prev_t, target_t, eps_t, low_w[0], rows, 1024, groups
+    )
+    w_attn = w_attn.reshape(width, -1)
+
+    relative = (neighbours - block_start + nodes) % (nodes * groups)
+    live = jnp.arange(NBR)[None, :] < nbr_count[:, None]
+    slots = jnp.where(live, relative, -1).reshape(nodes // GROUP, 256)
+    pad_enc = jnp.zeros((2, SLOT, width), bf16)
+    pad_enc = pad_enc.at[:, :VARS].set(w_enc.astype(bf16).reshape(2, VARS, width))
+    h_zero, norm_all, query, keyval, below, above, stat, counts = open_nodes(
+        node_in, pad_enc.reshape(2 * SLOT, width), modulation, stat, w_attn, slots, heads, groups, reach
+    )
+    norm_all, query, keyval, below, above = (
+        x.reshape(nodes, -1) for x in (norm_all, query, keyval, below, above)
+    )
+    stat_sum = stat[:, 0]
     count_sum = stat_sum[SLIM - 1]
     var_weight = 1.0 / (stat_sum[:VARS] / count_sum + norm_eps)
     loss_count = count_sum * VARS
-
-    pad_enc = jnp.zeros((2, SLOT, width), bf16)
-    pad_enc = pad_enc.at[:, :VARS].set(w_enc.astype(bf16).reshape(2, VARS, width))
-    h_zero, norm_one = enter(node_in, pad_enc.reshape(2 * SLOT, width), modulation)
-    norm_all = lax.all_gather(norm_one, "head", axis=0, tiled=True)
-    query, keyval = project(norm_all, w_attn, 512)
-    below = passed_along(keyval, "node", 1)
-    above = passed_along(keyval, "node", -1)
-
-    relative = (neighbours - block_start + nodes) % (nodes * groups)
-    live = jnp.arange(NBR)[None, :] < nbr_count[:, None]
-    slots = jnp.where(live, relative, -1).reshape(nodes // GROUP, 256)
-    counts = count_slots(slots, reach, 8)
-    e, mix, mixed_low = attend(query, below, keyval, above, counts, 128, 512)
-    mixed = lax.all_to_all(mixed_low.reshape(heads, rows, HD), "head", 0, 0)
+    e, mix, mixed = attend(query, below, keyval, above, counts, heads, 128, 512)
 
     w_dec_t = jnp.zeros((SLIM, width), bf16).at[:VARS].set(w_dec.T.astype(bf16))
     h_one, h_two, norm_two, up, act, dec = forward(mixed, h_zero, w_big, modulation, w_dec_t, 256)

time: 617 us -> 565 us (0.916)
  blocking collectives: 123 us -> 65.3 us
  Pallas kernels: 278 us -> 306 us
  waiting for transfers between devices: 113 us -> 95.6 us
  starting transfers between devices: 11.4 us -> 3.71 us
    pallas_call x3 -> x1, Pallas kernels: 18.5 us -> 65.4 us  [open_nodes(): pl.pallas_call(open_kernel, in_specs=[vmem()] * 6, out_specs=[vmem()] * 7...]
    psum x1 -> x0, blocking collectives: 39.7 us -> none  [local(): stat_sum = lax.psum(jnp.sum(stat, 1), 'node')]
    pallas_call x1, Pallas kernels: 75.1 us -> 36.5 us  [renew(): pl.pallas_call(renew_kernel, grid=(size // BLOCK,), in_specs=[whole(gram....]
    all_gather x1 -> x0, waiting for transfers between devices: 18.8 us -> none  [local(): norm_all = lax.all_gather(norm_one, 'head', axis=0, tiled=True)]
    all_gather x1 -> x0, blocking collectives: 17.6 us -> none  [local(): w_attn = lax.all_gather(low_w[0], 'node', axis=0, tiled=True)]
    pallas_call x1, Pallas kernels: 52.9 us -> 61.3 us  [settle(): pl.pallas_call(settle_kernel, in_specs=[smem()] + [pl.BlockSpec(memory_sp...]
    pallas_call x1, Pallas kernels: 35.7 us -> 42.4 us  [attend(): pl.pallas_call(functools.partial(attend_kernel, chunk=chunk), grid=(nodes...]
    ppermute x4 -> x2, waiting for transfers between devices: 42.4 us -> 42.7 us  [passed_along(): lax.ppermute(x, axis, [(i, (i + by) % length) for i in range(length)])]
  transfers between devices with their start and end apart: 9 -> 5, of which waited for: 6 -> 4; matrix products, arithmetic and copies ran while one was open for 4% -> 5% of each run, Pallas kernels for 16% -> 30%
where the time goes in v3:
time: 565 us; the launch traced here: 555 us
  Pallas kernels  306 us (54%)
  waiting for transfers between devices  95.6 us (17%)
  blocking collectives  65.3 us (12%)
  local copies, waits for them, and re-layouts  31.2 us (6%)
  between operations  19.8 us (4%)
  matrix products  19.2 us (3%)
  other arithmetic  14.1 us (2%)
    pallas_call x1, Pallas kernels, open_nodes(): pl.pallas_call(open_kernel, in_specs=[vmem()] * 6, out_specs=[vmem()] * 7...  65.4 us
    pallas_call x1, Pallas kernels, settle(): pl.pallas_call(settle_kernel, in_specs=[smem()] + [pl.BlockSpec(memory_sp...  61.3 us
    reduce_scatter x1, waiting for transfers between devices, local(): lax.psum_scatter(grad_big.reshape(heads * width, -1), both, scatter_dimen...  43.6 us
    ppermute x2, waiting for transfers between devices, passed_along(): lax.ppermute(x, axis, [(i, (i + by) % length) for i in range(length)])  42.7 us
    pallas_call x1, Pallas kernels, attend(): pl.pallas_call(functools.partial(attend_kernel, chunk=chunk), grid=(nodes...  42.4 us
    pallas_call x1, Pallas kernels, attend_back(): pl.pallas_call(functools.partial(attend_back_kernel, chunk=chunk), grid=(...  36.5 us
    pallas_call x1, Pallas kernels, renew(): pl.pallas_call(renew_kernel, grid=(size // BLOCK,), in_specs=[whole(gram....  36.5 us
    all_to_all x1, blocking collectives, local(): d_norm = lax.all_to_all(dn_part.reshape(heads, rows, width), 'head', 0, 0)  28.3 us
  transfers between devices with their start and end apart: 5, of which 4 were waited for; matrix products, arithmetic and copies ran while one was open for 5% of the time, Pallas kernels for 30%

profile of v3, /device:TPU:0, one launch (start us, length us, event | category | flops | bytes accessed | tf_op | source)
XLA Modules:
  0.0 555.2 jit_solution(12624500828784690223)
XLA Ops:
  22.9 2.3 copy-done.1
  25.1 16.2 %encode.1 = (f32[512,256]{1,0:T(8,128)S(1)}, f32[96,128]{1,0:T(8,128)S(1)}, bf16[8,64,512]{2,1,0:T(8,128)(2,1)S(1)}) custom-call(s32[4]{0:T(128)S(1)} %pad_add_fusion.place_ref, f32[2]{0:T(128)S(1)} %pad_maximum_fusion.2.scale_ref, s32[1,12288]{1,0:T(1,128)S(1)} %bitcast.140, f32[84,12288]{1,0:T(8,128)S(1)} %bitcast.128, f32[84,12288]{1,0:T(8,128)} %bitcast.144, ...), custom_call_target="tpu_custom_call" | custom-call | tf_op jit(solution)/shard_map/encode/pallas_call | solution.py:225
  43.6 65.4 %open_nodes.1 = (f32[512,512]{1,0:T(8,128)}, bf16[4,512,512]{2,1,0:T(8,128)(2,1)}, bf16[4,512,128]{2,1,0:T(8,128)(2,1)}, bf16[4,512,256]{2,1,0:T(8,128)(2,1)}, b...) custom-call(f32[512,256]{1,0:T(8,128)} %copy-done.8, ...), custom_call_target="tpu_custom_call" | custom-call | tf_op jit(solution)/shard_map/open_nodes/pallas_call | solution.py:361
  111.1 42.4 %attend.1 = (bf16[2048,6144]{1,0:T(8,128)(2,1)}, f32[2048,256]{1,0:T(8,128)}, bf16[4,512,128]{2,1,0:T(8,128)(2,1)}) custom-call(bf16[2048,128]{1,0:T(8,128)(2,1)} %bitcast.157, bf16[2048,256]{1,0:T(8,128)(2,1)} %bitcast.151, bf16[2048,256]{1,0:T(8,128)(2,1)} %bitcast.149, bf16[2048,256]{1,0:T(8,128)(2,1)} %bitcast.153, ...), custom_call_target="tpu_custom_call" | custom-call | tf_op jit(solution)/shard_map/attend/pallas_call | solution.py:473
  156.6 9.3 %forward.1 = (f32[512,512]{1,0:T(8,128)S(1)}, f32[512,512]{1,0:T(8,128)S(1)}, bf16[512,512]{1,0:T(8,128)(2,1)S(1)}, f32[4,512,512]{2,1,0:T(8,128)}, bf16[4,512,5...) custom-call(bf16[4,512,128]{2,1,0:T(8,128)(2,1)S(1)} %copy-done.10, f32[512,512]{1,0:T(8,128)S(1)} %copy-done.2, ...), custom_call_target="tpu_custom_call" | custom-call | tf_op jit(solution)/shard_map/forward/pallas_call | solution.py:582
  167.8 12.4 %all-gather = bf16[768,512]{1,0:T(8,128)(2,1)S(1)} all-gather(bf16[192,512]{1,0:T(8,128)(2,1)S(1)} %get-tuple-element.89), channel_id=2, replica_groups=mesh['head'=4,'node'=8] {'head'}, dimensions={0}, use_global_device_ids=true | all-gather | bytes 983040 | tf_op jit(solution)/shard_map/all_gather | solution.py:1105
  180.2 16.7 %pixels_back.1 = (f32[96,128]{1,0:T(8,128)S(1)}, f32[2048,128]{1,0:T(8,128)S(1)}) custom-call(s32[4]{0:T(128)S(1)} %pad_add_fusion.place_ref, f32[5]{0:T(128)S(1)} %stack.66.scale_ref, s32[1,12288]{1,0:T(1,128)S(1)} %bitcast.141, s32[3,12288]{1,0:T(4,128)S(1)} %bitcast.139, f32[84,12288]{1,0:T(8,128)} %bitcast.145, f32[84,12288]{1,0:T(8,128)} %bitcast.147, ...), custom_call_target="tpu_custom_call" | custom-call | tf_op jit(solution)/shard_map/pixels_back/pallas_call | solution.py:641
  196.9 13.3 %all_to_all.15.d_ref = f32[4,512,128]{2,1,0:T(8,128)} all-to-all(f32[4,512,128]{2,1,0:T(8,128)S(1)} %bitcast.133), channel_id=1, replica_groups=mesh['head'=4,'node'=8] {'head'}, dimensions={0} | all-to-all | bytes 2097152 | tf_op jit(solution)/shard_map/all_to_all | solution.py:1113
  210.3 17.0 %backward.1 = (f32[512,512]{1,0:T(8,128)}, bf16[4,512,128]{2,1,0:T(8,128)(2,1)}, f32[4,512,1152]{2,1,0:T(8,128)}, f32[96,512]{1,0:T(8,128)}, f32[8,512]{1,0:T(8,128)}) custom-call(f32[4,512,128]{2,1,0:T(8,128)} %all_to_all.15.d_ref, f32[512,512]{1,0:T(8,128)} %copy-done.13, f32[512,512]{1,0:T(8,128)} %copy-done.12, bf16[512,512]{1,0:T(8,128)(2,1)} %copy-done.19, ...), custom_call_target="tpu_custom_call" | custom-call | tf_op jit(solution)/shard_map/backward/pallas_call | solution.py:717
  227.4 11.3 %all_to_all.16 = bf16[4,512,128]{2,1,0:T(8,128)(2,1)} all-to-all(bf16[4,512,128]{2,1,0:T(8,128)(2,1)} %get-tuple-element.96), channel_id=1, replica_groups=mesh['head'=4,'node'=8] {'head'}, dimensions={0} | all-to-all | bytes 1048576 | tf_op jit(solution)/shard_map/all_to_all | solution.py:1120
  238.7 36.5 %attend_back.1 = (bf16[2048,128]{1,0:T(8,128)(2,1)}, bf16[256,2048]{1,0:T(8,128)(2,1)}, f32[256,2048]{1,0:T(8,128)}, bf16[256,2048]{1,0:T(8,128)(2,1)}) custom-call(bf16[2048,128]{1,0:T(8,128)(2,1)} %bitcast.158, bf16[2048,128]{1,0:T(8,128)(2,1)} %bitcast.159, f32[2048,256]{1,0:T(8,128)} %get-tuple-element.97.mix_ref, ...), custom_call_target="tpu_custom_call" | custom-call | tf_op jit(solution)/shard_map/attend_back/pallas_call | solution.py:537
  275.3 3.5 collective-permute-start.1
  278.8 32.6 %collective-permute-done.down_ref = bf16[256,2048]{1,0:T(8,128)(2,1)S(1)} collective-permute-done((bf16[256,2048]{1,0:T(8,128)(2,1)}, bf16[256,2048]{1,0:T(8,128)(2,1)S(1)}, u32[]{:S(2)}, u32[]{:S(2)}) %collective-permute-start) | collective-permute-done | bytes 1048608 | tf_op jit(solution)/shard_map/ppermute | solution.py:42
  311.5 10.1 %collective-permute-done.1.up_ref = bf16[256,2048]{1,0:T(8,128)(2,1)S(1)} collective-permute-done((bf16[256,2048]{1,0:T(8,128)(2,1)}, bf16[256,2048]{1,0:T(8,128)(2,1)S(1)}, u32[]{:S(2)}, u32[]{:S(2)}) %collective-permute-start.1) | collective-permute-done | bytes 1048608 | tf_op jit(solution)/shard_map/ppermute | solution.py:42
  322.6 4.9 unproject.1
  328.4 28.3 %all_to_all.17.dn_ref = bf16[4,512,512]{2,1,0:T(8,128)(2,1)} all-to-all(bf16[4,512,512]{2,1,0:T(8,128)(2,1)S(1)} %bitcast.132), channel_id=1, replica_groups=mesh['head'=4,'node'=8] {'head'}, dimensions={0} | all-to-all | bytes 4194304 | tf_op jit(solution)/shard_map/all_to_all | solution.py:1127
  356.7 43.6 %reduce-scatter.2.cloned.1.call-done.big_ref = f32[64,1152]{1,0:T(8,128)} async-done(((f32[2048,1152]{1,0:T(8,128)}), f32[64,1152]{1,0:T(8,128)}) %reduce-scatter.2.cloned.1.call-update) | async-done | bytes 294928 | tf_op jit(solution)/shard_map/reduce_scatter | solution.py:1117
  406.8 61.3 %settle.1 = (f32[256,512]{1,0:T(8,128)S(1)}, f32[64,384]{1,0:T(8,128)S(1)}, bf16[8,64,384]{2,1,0:T(8,128)(2,1)S(1)}, f32[8,128]{1,0:T(8,128)S(1)}) custom-call(f32[1]{0:T(128)} %bitcast.1.feat_ref, bf16[4,512,512]{2,1,0:T(8,128)(2,1)} %all_to_all.17.dn_ref, f32[512,512]{1,0:T(8,128)S(1)} %copy-done.3, f32[512,512]{1,0:T(8,128)S(1)} %copy-done.11, ...), custom_call_target="tpu_custom_call" | custom-call | tf_op jit(solution)/shard_map/settle/pallas_call | solution.py:918
  476.1 2.4 multiply_subtract_fusion
  480.8 3.9 fusion.17
  485.8 9.2 %all-gather.6.cloned.1.call-done = bf16[512,1152]{1,0:T(8,128)(2,1)} async-done(((bf16[64,1152]{1,0:T(8,128)(2,1)}), bf16[512,1152]{1,0:T(8,128)(2,1)}) %all-gather.6.cloned.1.call-update) | async-done | bytes 1179664 | tf_op jit(solution)/shard_map/all_gather | solution.py:1147
  498.7 5.3 fusion.product_ref
  504.0 5.4 fusion.58.gram_ref
  509.5 36.5 %renew.1 = f32[3,512,512]{2,1,0:T(8,128)} custom-call(f32[3,512,512]{2,1,0:T(8,128)S(1)} %fusion.58.gram_ref, f32[3,512,512]{2,1,0:T(8,128)} %copy-done.32), custom_call_target="tpu_custom_call" | custom-call | tf_op jit(solution)/shard_map/renew/pallas_call | solution.py:1013
  (134 shorter events, 45.4 us)
Async XLA Ops:
  7.2 471.4 %copy-start = (f32[3,1,512,512]{3,2,1,0:T(8,128)S(1)}, f32[3,1,512,512]{3,2,1,0:T(8,128)}, u32[]{:S(2)}) copy-start(f32[3,1,512,512]{3,2,1,0:T(8,128)} %param.42) | copy-start | bytes 9437188
  7.2 15.7 %copy-start.26 = (s32[12288]{0:T(1024)S(1)}, s32[12288]{0:T(1024)}, u32[]{:S(2)}) copy-start(s32[12288]{0:T(1024)} %param.34) | copy-start | bytes 147460
  7.2 147.1 %all-gather.4.cloned.1.call-start = ((), (), s32[]{:S(2)}) async-start(), calls=%async_computation.4 | async-start | bytes 4866048 | tf_op jit(solution)/shard_map/all_gather | solution.py:1067
  9.2 391.1 %reduce-scatter.2.cloned.1.call-start = ((), (), s32[]{:S(2)}) async-start(), calls=%async_computation.5 | async-start | bytes 9732096 | tf_op jit(solution)/shard_map/reduce_scatter | solution.py:1117
  25.1 85.1 %copy-start.38 = (f32[512,84]{0,1:T(8,128)S(1)}, f32[512,84]{0,1:T(8,128)}, u32[]{:S(2)}) copy-start(f32[512,84]{0,1:T(8,128)} %param.38) | copy-start | bytes 516100
  110.3 44.0 %copy-start.14 = (bf16[96,512]{1,0:T(8,128)(2,1)}, bf16[96,512]{1,0:T(8,128)(2,1)S(1)}, u32[]{:S(2)}) copy-start(bf16[96,512]{1,0:T(8,128)(2,1)S(1)} %scatter.9.wdec_ref) | copy-start | bytes 294916
  111.1 42.4 %copy-start.43 = (f32[96,128]{1,0:T(8,128)S(1)}, f32[96,128]{1,0:T(8,128)}, u32[]{:S(2)}) copy-start(f32[96,128]{1,0:T(8,128)} %get-tuple-element.82) | copy-start | bytes 147460
  111.1 43.2 %copy-start.22 = (f32[1,4,512]{2,1,0:T(4,128)S(1)}, f32[1,4,512]{2,1,0:T(4,128)}, u32[]{:S(2)}) copy-start(f32[1,4,512]{2,1,0:T(4,128)} %copy.70) | copy-start | bytes 24580
  156.6 23.6 %copy-start.25 = (s32[12288,3]{0,1:T(4,128)S(1)}, s32[12288,3]{0,1:T(4,128)}, u32[]{:S(2)}) copy-start(s32[12288,3]{0,1:T(4,128)} %param.35) | copy-start | bytes 442372
  167.8 29.1 %copy-start.19 = (bf16[512,512]{1,0:T(8,128)(2,1)}, bf16[512,512]{1,0:T(8,128)(2,1)S(1)}, u32[]{:S(2)}) copy-start(bf16[512,512]{1,0:T(8,128)(2,1)S(1)} %get-tuple-element.93.norm_ref) | copy-start | bytes 1572868
  196.9 13.4 %copy-start.28 = (f32[96,128]{1,0:T(8,128)}, f32[96,128]{1,0:T(8,128)S(1)}, u32[]{:S(2)}) copy-start(f32[96,128]{1,0:T(8,128)S(1)} %get-tuple-element.110.loss_ref) | copy-start | bytes 147460
  227.3 267.7 %all-gather.6.cloned.1.call-start = ((), (), s32[]{:S(2)}) async-start(), calls=%async_computation.6 | async-start | bytes 1327104 | tf_op jit(solution)/shard_map/all_gather | solution.py:1147
  238.7 82.8 %copy-start.7 = (bf16[8,64,512]{2,1,0:T(8,128)(2,1)S(1)}, bf16[8,64,512]{2,1,0:T(8,128)(2,1)}, u32[]{:S(2)}) copy-start(bf16[8,64,512]{2,1,0:T(8,128)(2,1)} %copy-done.6) | copy-start | bytes 1572868
  275.3 36.2 %collective-permute-start = (bf16[256,2048]{1,0:T(8,128)(2,1)}, bf16[256,2048]{1,0:T(8,128)(2,1)S(1)}, u32[]{:S(2)}, u32[]{:S(2)}) collective-permute-start(bf16[256,2048]{1,0:T(8,128)(2,1)} %get-tuple-element.101), channel_id=1, source_target_pairs={{0,1},{1,2},{2,3},{3,4},{4,5},{5,6},{6,7},{7,0},{8,9},{9,10},{10,1... | collective-permute-start | bytes 3145736 | tf_op jit(solution)/shard_map/ppermute | solution.py:42
  275.3 46.3 %collective-permute-start.1 = (bf16[256,2048]{1,0:T(8,128)(2,1)}, bf16[256,2048]{1,0:T(8,128)(2,1)S(1)}, u32[]{:S(2)}, u32[]{:S(2)}) collective-permute-start(bf16[256,2048]{1,0:T(8,128)(2,1)} %get-tuple-element.102), channel_id=1, source_target_pairs={{0,7},{1,0},{2,1},{3,2},{4,3},{5,4},{6,5},{7,6},{8,15},{9,8},{10,9... | collective-permute-start | bytes 3145736 | tf_op jit(solution)/shard_map/ppermute | solution.py:42
  328.4 71.9 %copy-start.23 = (f32[1,4,512]{2,1,0:T(4,128)S(1)}, f32[1,4,512]{2,1,0:T(4,128)}, u32[]{:S(2)}) copy-start(f32[1,4,512]{2,1,0:T(4,128)} %copy.70) | copy-start | bytes 24580
  328.4 71.9 %copy-start.29 = (f32[96,128]{1,0:T(8,128)S(1)}, f32[96,128]{1,0:T(8,128)}, u32[]{:S(2)}) copy-start(f32[96,128]{1,0:T(8,128)} %copy-done.28) | copy-start | bytes 147460
  328.4 71.9 %copy-start.31 = (f32[8,512]{1,0:T(8,128)S(1)}, f32[8,512]{1,0:T(8,128)}, u32[]{:S(2)}) copy-start(f32[8,512]{1,0:T(8,128)} %get-tuple-element.107.gmod_ref) | copy-start | bytes 49156
  406.8 66.3 %slice-start = ((f32[64,1152]{1,0:T(8,128)}), f32[64,128]{1,0:T(8,128)S(1)}, s32[]{:S(2)}) async-start(f32[64,1152]{1,0:T(8,128)} %reduce-scatter.2.cloned.1.call-done.big_ref), calls=%async_computation.7 | async-start | bytes 65536 | tf_op jit(solution)/shard_map/slice | solution.py:1138
  406.8 67.2 %copy-start.5 = (f32[64,1152]{1,0:T(8,128)S(1)}, f32[64,1152]{1,0:T(8,128)}, u32[]{:S(2)}) copy-start(f32[64,1152]{1,0:T(8,128)} %reduce-scatter.2.cloned.1.call-done.big_ref) | copy-start | bytes 884740
  472.3 6.3 %copy-start.39 = (f32[3,64,512]{2,1,0:T(8,128)S(1)}, f32[3,64,512]{2,1,0:T(8,128)}, u32[]{:S(2)}) copy-start(f32[3,64,512]{2,1,0:T(8,128)} %param.40) | copy-start | bytes 1179652
  472.3 6.3 %copy-start.40 = (f32[3,64,512]{2,1,0:T(8,128)S(1)}, f32[3,64,512]{2,1,0:T(8,128)}, u32[]{:S(2)}) copy-start(f32[3,64,512]{2,1,0:T(8,128)} %param.41) | copy-start | bytes 1179652
  480.7 15.3 %copy-start.21 = (bf16[8,64,384]{2,1,0:T(8,128)(2,1)S(1)}, bf16[8,64,384]{2,1,0:T(8,128)(2,1)}, u32[]{:S(2)}) copy-start(bf16[8,64,384]{2,1,0:T(8,128)(2,1)} %copy-done.20) | copy-start | bytes 1179652
  504.0 5.5 copy-start.32
  (27 other events, 49.1 us)
Sparse Core Ops, SparseCore 0:
  11.6 84.3 all-gather.3
  227.5 172.7 reduce-scatter.1
  472.4 22.5 all-gather.5
